TPU v7x, 512 devices: a whole 4x4x16 slice. The times are simulated.
512 devices in a mesh: dp: 64 (over z, y_hi, core), mp: 8 (over y_lo, x).
Axes of the slice: x: 4, y: 4 (y_hi: 2, y_lo: 2; y = y_hi * 2 + y_lo), z: 16, core: 2. Of those that a mesh axis runs over, the one named last changes fastest.
Arguments:
- inputs: float32 [512, 6144], P('dp', 'mp'), may hold values from -6 to 6
- w_in: float32 [6144, 24576], P('mp', 'dp'), may hold values from -0.078125 to 0.078125
- w_out: float32 [24576, 6144], P('dp', 'mp'), may hold values from -0.0390625 to 0.0390625
- cotangent: float32 [512, 6144], P('dp', 'mp'), may hold values from -6 to 6
Outputs:
- output: float32 [512, 6144], P('dp', 'mp')
- input_grad: float32 [512, 6144], P('dp', 'mp')
- w_in_grad: float32 [6144, 24576], P('mp', 'dp')
- w_out_grad: float32 [24576, 6144], P('dp', 'mp')
All inputs are finite; a program needn't handle non-finite values.
Results may differ from a plain program's by a relative error of at most 0.000088.
Values sent between devices are 32-bit elements; how exact they have to be, the bound alone decides.
No kernel may reach another device: no remote copies, remote signals or barrier semaphores. Data moves between devices by JAX's collectives and lax.ppermute only.
A program may use at most 64 MiB of HBM per device.

v0:
```python
from functools import partial

import jax
import jax.numpy as jnp
from jax import lax
from jax.sharding import PartitionSpec as P


def shards(inputs, w_in, w_out, cotangent):
    highest = lax.Precision.HIGHEST
    gelu_fn = partial(jax.nn.gelu, approximate=True)
    local_rows = inputs.shape[0]
    gathered = lax.all_gather(inputs, "dp", axis=0, tiled=True)
    summand = jnp.dot(gathered, w_in, precision=highest, preferred_element_type=jnp.float32)
    hidden = lax.psum(summand, "mp")
    activated, gelu_back = jax.vjp(gelu_fn, hidden)
    picked = lax.slice_in_dim(activated, 0, local_rows * lax.axis_size("dp"), axis=0)
    output = lax.psum_scatter(
        jnp.dot(picked, w_out, precision=highest, preferred_element_type=jnp.float32),
        "dp",
        scatter_dimension=0,
        tiled=True,
    )
    grad_all = lax.all_gather(cotangent, "dp", axis=0, tiled=True)
    w_out_grad = jnp.einsum("tf,td->fd", activated, grad_all, precision=highest)
    grad_term = jnp.einsum("td,fd->tf", grad_all, w_out, precision=highest)
    act_grad = lax.psum(grad_term, "mp")
    hid_grad = gelu_back(act_grad)[0]
    w_in_grad = jnp.einsum("td,tf->df", gathered, hid_grad, precision=highest)
    picked = hid_grad
    input_grad = lax.psum_scatter(
        jnp.einsum("tf,df->td", picked, w_in, precision=highest),
        "dp",
        scatter_dimension=0,
        tiled=True,
    )
    return (output, input_grad, w_in_grad, w_out_grad)


def solution(mesh):
    placed = (P("dp", "mp"), P("mp", "dp"), P("dp", "mp"), P("dp", "mp"))
    return jax.shard_map(
        shards,
        mesh=mesh,
        in_specs=placed,
        out_specs=(P("dp", "mp"), P("dp", "mp"), P("mp", "dp"), P("dp", "mp")),
        check_vma=False,
    )
```

profile of v0, /device:TPU:4, one launch (start us, length us, event | category | flops | bytes accessed | tf_op | source)
XLA Modules:
  0.0 831.9 jit_solution(12869552231341351327)
XLA Ops:
  7.2 0.0 all-gather.5.cloned.1.call-start
  7.2 0.7 all-gather.5.cloned.1.call-update
  7.9 0.0 all-gather.3.cloned.1.call-start
  8.0 0.7 all-gather.3.cloned.1.call-update
  8.7 0.0 all-reduce.3.cloned.1.call-start
  8.7 149.1 %all-gather.5.cloned.1.call-done = f32[512,768]{1,0:T(8,128)} async-done(((f32[8,768]{1,0:T(8,128)}), f32[512,768]{1,0:T(8,128)}) %all-gather.5.cloned.1.call-update) | async-done | bytes 1572880 | tf_op jit(solution)/shard_map/all_gather | solution.py:24
  157.8 5.3 fusion.20
  163.1 134.4 %all-gather.3.cloned.1.call-done = f32[512,768]{1,0:T(8,128)} async-done(((f32[8,768]{1,0:T(8,128)}), f32[512,768]{1,0:T(8,128)}) %all-gather.3.cloned.1.call-update) | async-done | bytes 1572880 | tf_op jit(solution)/shard_map/all_gather | solution.py:13
  297.5 4.9 fusion.19
  302.4 0.0 all-reduce.3.cloned.1.call-update
  302.4 0.0 reduce-scatter.5.cloned.1.call-start
  302.5 88.0 %all-reduce.3.cloned.1.call-done = (f32[512,384]{1,0:T(8,128)}, f32[512,384]{1,0:T(8,128)}) async-done(((f32[512,384]{1,0:T(8,128)}, f32[512,384]{1,0:T(8,128)}), (f32[512,384]{1,0:T(8,128)}, f32[512,384]{1,0:T(8,128)})) %all-reduce.3.cloned.1.call-update) | async-done | bytes 1572880 | tf_op jit(solution)/shard_map/psum | solution.py:15
  390.5 5.7 fusion.17
  396.3 0.0 reduce-scatter.5.cloned.1.call-update
  396.3 0.2 reduce-scatter.3.cloned.1.call-start
  396.5 1.0 copy-done.2
  397.5 4.0 fusion.7
  401.6 0.0 reduce-scatter.3.cloned.1.call-update
  401.6 1.4 copy-done.4
  403.0 4.8 convolution_bitcast_fusion
  407.7 2.8 copy.8
  410.5 3.3 fusion.6
  413.9 196.6 %reduce-scatter.5.cloned.1.call-done = f32[8,768]{1,0:T(8,128)} async-done(((f32[512,768]{1,0:T(8,128)}), f32[8,768]{1,0:T(8,128)}) %reduce-scatter.5.cloned.1.call-update) | async-done | bytes 24592 | tf_op jit(solution)/shard_map/reduce_scatter | solution.py:31
  610.5 214.9 %reduce-scatter.3.cloned.1.call-done = f32[8,768]{1,0:T(8,128)} async-done(((f32[512,768]{1,0:T(8,128)}), f32[8,768]{1,0:T(8,128)}) %reduce-scatter.3.cloned.1.call-update) | async-done | bytes 24592 | tf_op jit(solution)/shard_map/reduce_scatter | solution.py:18
  (8 shorter events, 0.0 us)
Async XLA Ops:
  7.2 290.3 %copy-start = (f32[768,384]{1,0:T(8,128)S(1)}, f32[768,384]{1,0:T(8,128)}, u32[]{:S(2)}) copy-start(f32[768,384]{1,0:T(8,128)} %param.5) | copy-start | bytes 3538948
  7.2 150.6 %all-gather.5.cloned.1.call-start = ((), (), s32[]{:S(2)}) async-start(), calls=%async_computation.4 | async-start | bytes 1597440 | tf_op jit(solution)/shard_map/all_gather | solution.py:24
  7.9 289.6 %all-gather.3.cloned.1.call-start = ((), (), s32[]{:S(2)}) async-start(), calls=%async_computation.2 | async-start | bytes 1597440 | tf_op jit(solution)/shard_map/all_gather | solution.py:13
  8.7 381.8 %all-reduce.3.cloned.1.call-start = ((), (), s32[]{:S(2)}) async-start(), calls=%async_computation.6 | async-start | bytes 3145728 | tf_op jit(solution)/shard_map/psum | solution.py:15
  302.4 308.1 %reduce-scatter.5.cloned.1.call-start = ((), (), s32[]{:S(2)}) async-start(), calls=%async_computation.5 | async-start | bytes 1597440 | tf_op jit(solution)/shard_map/reduce_scatter | solution.py:31
  390.5 6.0 copy-start.3
  396.3 1.3 copy-start.2
  396.3 429.1 %reduce-scatter.3.cloned.1.call-start = ((), (), s32[]{:S(2)}) async-start(), calls=%async_computation.3 | async-start | bytes 1597440 | tf_op jit(solution)/shard_map/reduce_scatter | solution.py:18
  401.6 1.4 copy-start.4
  407.7 2.8 copy-start.1
Sparse Core Ops, SparseCore 0:
  11.3 146.4 all-gather.4
  161.1 136.3 all-gather.2
  302.5 87.9 all-reduce.2
  396.4 214.0 reduce-scatter.4
  615.6 209.7 reduce-scatter.2
where the time goes:
time: 832 us
  waiting for transfers between devices  784 us (94%)
  matrix products  28.1 us (3%)
  between operations  13.8 us (2%)
    reduce_scatter x1, waiting for transfers between devices, shards(): lax.psum_scatter(jnp.dot(picked, w_out, precision=highest, preferred_elem...  215 us
    reduce_scatter x1, waiting for transfers between devices, shards(): lax.psum_scatter(jnp.einsum('tf,df->td', picked, w_in, precision=highest)...  197 us
    all_gather x1, waiting for transfers between devices, shards(): grad_all = lax.all_gather(cotangent, 'dp', axis=0, tiled=True)  149 us
    all_gather x1, waiting for transfers between devices, shards(): gathered = lax.all_gather(inputs, 'dp', axis=0, tiled=True)  134 us
    psum x1, waiting for transfers between devices, shards(): hidden = lax.psum(summand, 'mp')  88 us
  transfers between devices with their start and end apart: 5, of which 5 were waited for; matrix products, arithmetic and copies ran while one was open for 2% of the time, Pallas kernels for 0%

commit v1 on v0

v1 whole, which is shorter than its diff:
```python
from functools import partial

import jax
import jax.numpy as jnp
from jax import lax
from jax.sharding import PartitionSpec as P

NZ, NY, NC = 16, 2, 2
Z_GROUPS = [[z * NY * NC + q for z in range(NZ)] for q in range(NY * NC)]
CORE_SWAP = [(d, d ^ 1) for d in range(NZ * NY * NC)]
Y_SWAP = [(d, d ^ 2) for d in range(NZ * NY * NC)]

dot = partial(lax.dot_general, precision=lax.Precision.HIGH, preferred_element_type=jnp.float32)


def mm(a, b):
    return dot(a, b, (((1,), (0,)), ((), ())))


def mm_nt(a, b):
    return dot(a, b, (((1,), (1,)), ((), ())))


def mm_tn(a, b):
    return dot(a, b, (((0,), (0,)), ((), ())))


def spread(part):
    mine = jnp.concatenate([part, lax.ppermute(part, "dp", Y_SWAP)], axis=0)
    return jnp.concatenate([mine, lax.ppermute(mine, "dp", CORE_SWAP)], axis=0)


def sum_mp(term):
    n = lax.axis_size("mp")
    got = lax.all_to_all(term, "mp", 0, 0, tiled=True)
    return got.reshape(n, term.shape[0] // n, term.shape[1]).sum(0)


def gather_mp(part):
    copies = jnp.tile(part, (lax.axis_size("mp"), 1))
    return lax.all_to_all(copies, "mp", 0, 0, tiled=True)


def scatter_dp(term):
    half = term.shape[0] // 2
    term = term[:half] + lax.ppermute(term[half:], "dp", CORE_SWAP)
    half //= 2
    term = term[:half] + lax.ppermute(term[half:], "dp", Y_SWAP)
    got = lax.all_to_all(term, "dp", 0, 0, tiled=True, axis_index_groups=Z_GROUPS)
    return got.reshape(NZ, half // NZ, term.shape[1]).sum(0)


def shards(inputs, w_in, w_out, cotangent):
    gelu_fn = partial(jax.nn.gelu, approximate=True)
    rows, width = inputs.shape
    both = jnp.concatenate([inputs, cotangent], axis=0)
    ring = lax.all_gather(both, "dp", axis=0, axis_index_groups=Z_GROUPS)
    tokens = spread(ring[:, :rows].reshape(NZ * rows, width))
    hidden = sum_mp(mm(tokens, w_in))
    grads = spread(ring[:, rows:].reshape(NZ * rows, width))
    act_grad = sum_mp(mm_nt(grads, w_out))
    activated, gelu_back = jax.vjp(gelu_fn, hidden)
    hid_grad = gelu_back(act_grad)[0]
    activated = gather_mp(activated)
    hid_grad = gather_mp(hid_grad)
    output = scatter_dp(mm(activated, w_out))
    input_grad = scatter_dp(mm_nt(hid_grad, w_in))
    w_out_grad = mm_tn(activated, grads)
    w_in_grad = mm_tn(tokens, hid_grad)
    return (output, input_grad, w_in_grad, w_out_grad)


def solution(mesh):
    placed = (P("dp", "mp"), P("mp", "dp"), P("dp", "mp"), P("dp", "mp"))
    return jax.shard_map(
        shards,
        mesh=mesh,
        in_specs=placed,
        out_specs=(P("dp", "mp"), P("dp", "mp"), P("mp", "dp"), P("dp", "mp")),
        check_vma=False,
    )
```

time: 832 us -> 224 us (0.27)
  the two profiles are of different devices: /device:TPU:4 before, /device:TPU:2 now
where the time goes in v1:
time: 224 us; the launch traced here: 223 us
  waiting for transfers between devices  79.7 us (36%)
  blocking collectives  55.6 us (25%)
  starting transfers between devices  52.8 us (24%)
  matrix products  15.8 us (7%)
  other arithmetic  11.9 us (5%)
  local copies, waits for them, and re-layouts  6.31 us (3%)
    all_gather x1, blocking collectives, shards(): ring = lax.all_gather(both, 'dp', axis=0, axis_index_groups=Z_GROUPS)  40.1 us
    all_to_all x2, waiting for transfers between devices, scatter_dp(): lax.all_to_all(term, 'dp', 0, 0, tiled=True, axis_index_groups=Z_GROUPS)  24.3 us
    all_to_all x2, waiting for transfers between devices, sum_mp(): got = lax.all_to_all(term, 'mp', 0, 0, tiled=True)  19.8 us
    ppermute x2, waiting for transfers between devices, spread(): mine = jnp.concatenate([part, lax.ppermute(part, 'dp', Y_SWAP)], axis=0)  15.9 us
    all_to_all x1, blocking collectives, gather_mp(): return lax.all_to_all(copies, 'mp', 0, 0, tiled=True)  15.5 us
    ppermute x2, waiting for transfers between devices, scatter_dp(): term = term[:half] + lax.ppermute(term[half:], 'dp', Y_SWAP)  14.2 us
    all_to_all x2, starting transfers between devices, scatter_dp(): lax.all_to_all(term, 'dp', 0, 0, tiled=True, axis_index_groups=Z_GROUPS)  12.5 us
    all_to_all x2, starting transfers between devices, sum_mp(): got = lax.all_to_all(term, 'mp', 0, 0, tiled=True)  10.6 us
  transfers between devices with their start and end apart: 13, of which 9 were waited for; matrix products, arithmetic and copies ran while one was open for 12% of the time, Pallas kernels for 0%

profile of v1, /device:TPU:2, one launch (start us, length us, event | category | flops | bytes accessed | tf_op | source)
XLA Modules:
  0.0 223.1 jit_solution(18072438988988305057)
XLA Ops:
  1.5 40.1 %all-gather = f32[256,768]{1,0:T(8,128)S(1)} all-gather(f32[16,768]{1,0:T(8,128)S(1)} %pad_maximum_fusion.8), channel_id=2, replica_groups={{0,32,64,96,128,160,192,224,256,288,320,352,384,416,448,480},{8,40,72,1..., dimensions={0}, use_global_device_ids=true | all-gather | bytes 835584 | tf_op jit(solution)/shard_map/all_gather | solution.py:57
  41.7 5.1 %collective-permute-start.4 = (f32[128,768]{1,0:T(8,128)S(1)}, f32[128,768]{1,0:T(8,128)S(1)}, u32[]{:S(2)}, u32[]{:S(2)}) collective-permute-start(f32[128,768]{1,0:T(8,128)S(1)} %get-tuple-element.4), channel_id=1, source_target_pairs={{0,16},{8,24},{16,0},{24,8},{32,48},{40,56},{48,32},{56,40},{64,80... | collective-permute-start | bytes 1179656 | tf_op jit(solution)/shard_map/ppermute | solution.py:29
  46.8 6.1 %collective-permute-done.4 = f32[128,768]{1,0:T(8,128)S(1)} collective-permute-done((f32[128,768]{1,0:T(8,128)S(1)}, f32[128,768]{1,0:T(8,128)S(1)}, u32[]{:S(2)}, u32[]{:S(2)}) %collective-permute-start.4) | collective-permute-done | bytes 393248 | tf_op jit(solution)/shard_map/ppermute | solution.py:29
  54.8 5.1 %collective-permute-start = (f32[128,768]{1,0:T(8,128)S(1)}, f32[128,768]{1,0:T(8,128)S(1)}, u32[]{:S(2)}, u32[]{:S(2)}) collective-permute-start(f32[128,768]{1,0:T(8,128)S(1)} %get-tuple-element.5), channel_id=1, source_target_pairs={{0,16},{8,24},{16,0},{24,8},{32,48},{40,56},{48,32},{56,40},{64,80... | collective-permute-start | bytes 1179656 | tf_op jit(solution)/shard_map/ppermute | solution.py:29
  59.9 9.8 %collective-permute-done = f32[128,768]{1,0:T(8,128)S(1)} collective-permute-done((f32[128,768]{1,0:T(8,128)S(1)}, f32[128,768]{1,0:T(8,128)S(1)}, u32[]{:S(2)}, u32[]{:S(2)}) %collective-permute-start) | collective-permute-done | bytes 393248 | tf_op jit(solution)/shard_map/ppermute | solution.py:29
  72.7 2.3 %fusion.1 = f32[512,384]{1,0:T(8,128)} fusion(f32[384,768]{1,0:T(8,128)S(1)} %copy-done, f32[256,768]{1,0:T(8,128)S(1)} %collective-permute-done.5, f32[128,768]{1,0:T(8,128)S(1)} %collective-permute-done.4, f32[128,768]{1,0:T(8,128)S(1)} %get-tuple-element.4), kind=kOutput, calls=%fused_computation.3 | convolution fusion | flops 906756096 | bytes 3538944 | tf_op jit(solution)/shard_map/dot_general | solution.py:21
  75.0 6.0 %all-to-all-start.3 = ((f32[8,64,384]{2,1,0:T(8,128)}), f32[8,64,384]{2,1,0:T(8,128)}, u32[]{:S(2)}, u32[]{:S(2)}) async-start(f32[8,64,384]{2,1,0:T(8,128)} %bitcast.26), calls=%async_computation.3 | async-start | bytes 1572864 | tf_op jit(solution)/shard_map/all_to_all | solution.py:35
  81.0 3.4 %fusion.3 = f32[512,384]{1,0:T(8,128)} fusion(f32[768,384]{1,0:T(8,128)S(1)} %copy-done.3, f32[256,768]{1,0:T(8,128)} %collective-permute-done.1, f32[128,768]{1,0:T(8,128)S(1)} %collective-permute-done, f32[128,768]{1,0:T(8,128)S(1)} %get-tuple-element.5), kind=kOutput, calls=%fused_computation.5 | convolution fusion | flops 906756096 | bytes 3538944 | tf_op jit(solution)/shard_map/dot_general | solution.py:17
  84.4 9.1 %all-to-all-done.3 = f32[8,64,384]{2,1,0:T(8,128)} async-done(((f32[8,64,384]{2,1,0:T(8,128)}), f32[8,64,384]{2,1,0:T(8,128)}, u32[]{:S(2)}, u32[]{:S(2)}) %all-to-all-start.3) | async-done | bytes 786464 | tf_op jit(solution)/shard_map/all_to_all | solution.py:35
  93.5 4.6 %all-to-all-start = ((f32[8,64,384]{2,1,0:T(8,128)}), f32[8,64,384]{2,1,0:T(8,128)S(1)}, u32[]{:S(2)}, u32[]{:S(2)}) async-start(f32[8,64,384]{2,1,0:T(8,128)} %bitcast.25), calls=%async_computation | async-start | bytes 1572864 | tf_op jit(solution)/shard_map/all_to_all | solution.py:35
  99.3 10.8 %all-to-all-done = f32[8,64,384]{2,1,0:T(8,128)S(1)} async-done(((f32[8,64,384]{2,1,0:T(8,128)}), f32[8,64,384]{2,1,0:T(8,128)S(1)}, u32[]{:S(2)}, u32[]{:S(2)}) %all-to-all-start) | async-done | bytes 786464 | tf_op jit(solution)/shard_map/all_to_all | solution.py:35
  110.2 15.5 %all_to_all.54 = f32[8,64,384]{2,1,0:T(8,128)S(1)} all-to-all(f32[8,64,384]{2,1,0:T(8,128)S(1)} %tile.4), channel_id=1, replica_groups=mesh['dp'=64,'mp'=8] {'mp'}, dimensions={0} | all-to-all | bytes 1572864 | tf_op jit(solution)/shard_map/all_to_all | solution.py:41
  132.1 4.6 %all-to-all-start.4 = ((f32[8,64,384]{2,1,0:T(8,128)}), f32[8,64,384]{2,1,0:T(8,128)S(1)}, u32[]{:S(2)}, u32[]{:S(2)}) async-start(f32[8,64,384]{2,1,0:T(8,128)} %tile.5), calls=%async_computation.4 | async-start | bytes 1572864 | tf_op jit(solution)/shard_map/all_to_all | solution.py:41
  139.1 4.8 %collective-permute-start.3 = (f32[128,768]{1,0:T(8,128)}, f32[128,768]{1,0:T(8,128)}, u32[]{:S(2)}, u32[]{:S(2)}) collective-permute-start(f32[128,768]{1,0:T(8,128)} %slice.44), channel_id=1, source_target_pairs={{0,16},{8,24},{16,0},{24,8},{32,48},{40,56},{48,32},{56,40},{64,80... | collective-permute-start | bytes 1179656 | tf_op jit(solution)/shard_map/ppermute | solution.py:48
  144.0 5.4 %all-to-all-done.4 = f32[8,64,384]{2,1,0:T(8,128)S(1)} async-done(((f32[8,64,384]{2,1,0:T(8,128)}), f32[8,64,384]{2,1,0:T(8,128)S(1)}, u32[]{:S(2)}, u32[]{:S(2)}) %all-to-all-start.4) | async-done | bytes 786464 | tf_op jit(solution)/shard_map/all_to_all | solution.py:41
  149.4 2.7 %fusion.17 = f32[512,768]{1,0:T(8,128)S(1)} fusion(f32[512,384]{1,0:T(8,128)S(1)} %bitcast.23, f32[768,384]{1,0:T(8,128)} %param.5), kind=kOutput, calls=%fused_computation.31 | convolution fusion | flops 905969664 | bytes 3538944 | tf_op jit(solution)/shard_map/dot_general | solution.py:21
  156.1 2.6 %collective-permute-done.3 = f32[128,768]{1,0:T(8,128)} collective-permute-done((f32[128,768]{1,0:T(8,128)}, f32[128,768]{1,0:T(8,128)}, u32[]{:S(2)}, u32[]{:S(2)}) %collective-permute-start.3) | collective-permute-done | bytes 393248 | tf_op jit(solution)/shard_map/ppermute | solution.py:48
  160.5 6.7 %all-to-all-start.2 = ((f32[16,8,768]{2,1,0:T(8,128)}), f32[16,8,768]{2,1,0:T(8,128)}, u32[]{:S(2)}, u32[]{:S(2)}) async-start(f32[16,8,768]{2,1,0:T(8,128)} %fusion.5), calls=%async_computation.2 | async-start | bytes 786432 | tf_op jit(solution)/shard_map/all_to_all | solution.py:49
  168.7 2.5 %collective-permute-start.7 = (f32[128,768]{1,0:T(8,128)S(1)}, f32[128,768]{1,0:T(8,128)S(1)}, u32[]{:S(2)}, u32[]{:S(2)}) collective-permute-start(f32[128,768]{1,0:T(8,128)S(1)} %slice.49), channel_id=1, source_target_pairs={{0,16},{8,24},{16,0},{24,8},{32,48},{40,56},{48,32},{56,40},{64,80... | collective-permute-start | bytes 1179656 | tf_op jit(solution)/shard_map/ppermute | solution.py:48
  171.3 11.6 %collective-permute-done.7 = f32[128,768]{1,0:T(8,128)S(1)} collective-permute-done((f32[128,768]{1,0:T(8,128)S(1)}, f32[128,768]{1,0:T(8,128)S(1)}, u32[]{:S(2)}, u32[]{:S(2)}) %collective-permute-start.7) | collective-permute-done | bytes 393248 | tf_op jit(solution)/shard_map/ppermute | solution.py:48
  183.7 7.8 %all-to-all-done.2 = f32[16,8,768]{2,1,0:T(8,128)} async-done(((f32[16,8,768]{2,1,0:T(8,128)}), f32[16,8,768]{2,1,0:T(8,128)}, u32[]{:S(2)}, u32[]{:S(2)}) %all-to-all-start.2) | async-done | bytes 393248 | tf_op jit(solution)/shard_map/all_to_all | solution.py:49
  191.5 5.8 %all-to-all-start.5 = ((f32[16,8,768]{2,1,0:T(8,128)}), f32[16,8,768]{2,1,0:T(8,128)}, u32[]{:S(2)}, u32[]{:S(2)}) async-start(f32[16,8,768]{2,1,0:T(8,128)} %fusion.4), calls=%async_computation.5 | async-start | bytes 786432 | tf_op jit(solution)/shard_map/all_to_all | solution.py:49
  197.3 3.8 %fusion.2 = f32[768,384]{1,0:T(8,128)} fusion(f32[512,384]{1,0:T(8,128)S(1)} %bitcast.24, f32[256,768]{1,0:T(8,128)} %collective-permute-done.1, f32[128,768]{1,0:T(8,128)} %copy-done.6, f32[128,768]{1,0:T(8,128)S(1)} %get-tuple-element.5), kind=kOutput, calls=%fused_computation.4 | convolution fusion | flops 906756096 | bytes 3538944 | tf_op jit(solution)/shard_map/dot_general | solution.py:25
  205.0 16.5 %all-to-all-done.5 = f32[16,8,768]{2,1,0:T(8,128)} async-done(((f32[16,8,768]{2,1,0:T(8,128)}), f32[16,8,768]{2,1,0:T(8,128)}, u32[]{:S(2)}, u32[]{:S(2)}) %all-to-all-start.5) | async-done | bytes 393248 | tf_op jit(solution)/shard_map/all_to_all | solution.py:49
  (51 shorter events, 29.6 us)
Async XLA Ops:
  0.6 72.0 %copy-start = (f32[384,768]{1,0:T(8,128)S(1)}, f32[384,768]{1,0:T(8,128)}, u32[]{:S(2)}) copy-start(f32[384,768]{1,0:T(8,128)} %param.6) | copy-start | bytes 3538948
  41.7 11.2 %collective-permute-start.4 = (f32[128,768]{1,0:T(8,128)S(1)}, f32[128,768]{1,0:T(8,128)S(1)}, u32[]{:S(2)}, u32[]{:S(2)}) collective-permute-start(f32[128,768]{1,0:T(8,128)S(1)} %get-tuple-element.4), channel_id=1, source_target_pairs={{0,16},{8,24},{16,0},{24,8},{32,48},{40,56},{48,32},{56,40},{64,80... | collective-permute-start | bytes 1179656 | tf_op jit(solution)/shard_map/ppermute | solution.py:29
  52.8 19.8 %copy-start.4 = (f32[128,768]{1,0:T(8,128)}, f32[128,768]{1,0:T(8,128)S(1)}, u32[]{:S(2)}) copy-start(f32[128,768]{1,0:T(8,128)S(1)} %collective-permute-done.4) | copy-start | bytes 1179652
  52.9 19.7 %collective-permute-start.5 = (f32[256,768]{1,0:T(8,128)S(1)}, f32[256,768]{1,0:T(8,128)S(1)}, u32[]{:S(2)}, u32[]{:S(2)}) collective-permute-start(f32[256,768]{1,0:T(8,128)S(1)} %pad_maximum_fusion.7), channel_id=1, source_target_pairs={{0,8},{8,0},{16,24},{24,16},{32,40},{40,32},{48,56},{56,48},{64,72... | collective-permute-start | bytes 2359304 | tf_op jit(solution)/shard_map/ppermute | solution.py:30
  54.8 14.9 %collective-permute-start = (f32[128,768]{1,0:T(8,128)S(1)}, f32[128,768]{1,0:T(8,128)S(1)}, u32[]{:S(2)}, u32[]{:S(2)}) collective-permute-start(f32[128,768]{1,0:T(8,128)S(1)} %get-tuple-element.5), channel_id=1, source_target_pairs={{0,16},{8,24},{16,0},{24,8},{32,48},{40,56},{48,32},{56,40},{64,80... | collective-permute-start | bytes 1179656 | tf_op jit(solution)/shard_map/ppermute | solution.py:29
  69.8 11.2 %copy-start.6 = (f32[128,768]{1,0:T(8,128)}, f32[128,768]{1,0:T(8,128)S(1)}, u32[]{:S(2)}) copy-start(f32[128,768]{1,0:T(8,128)S(1)} %collective-permute-done) | copy-start | bytes 1179652
  70.7 10.2 %collective-permute-start.1 = (f32[256,768]{1,0:T(8,128)}, f32[256,768]{1,0:T(8,128)}, u32[]{:S(2)}, u32[]{:S(2)}) collective-permute-start(f32[256,768]{1,0:T(8,128)} %pad_maximum_fusion.6), channel_id=1, source_target_pairs={{0,8},{8,0},{16,24},{24,16},{32,40},{40,32},{48,56},{56,48},{64,72... | collective-permute-start | bytes 2359304 | tf_op jit(solution)/shard_map/ppermute | solution.py:30
  72.7 2.3 %copy-start.7 = (f32[256,768]{1,0:T(8,128)}, f32[256,768]{1,0:T(8,128)S(1)}, u32[]{:S(2)}) copy-start(f32[256,768]{1,0:T(8,128)S(1)} %collective-permute-done.5) | copy-start | bytes 2359300
  75.0 6.0 %copy-start.3 = (f32[768,384]{1,0:T(8,128)S(1)}, f32[768,384]{1,0:T(8,128)}, u32[]{:S(2)}) copy-start(f32[768,384]{1,0:T(8,128)} %param.5) | copy-start | bytes 3538948
  75.0 18.5 %all-to-all-start.3 = ((f32[8,64,384]{2,1,0:T(8,128)}), f32[8,64,384]{2,1,0:T(8,128)}, u32[]{:S(2)}, u32[]{:S(2)}) async-start(f32[8,64,384]{2,1,0:T(8,128)} %bitcast.26), calls=%async_computation.3 | async-start | bytes 1572864 | tf_op jit(solution)/shard_map/all_to_all | solution.py:35
  93.5 16.6 %all-to-all-start = ((f32[8,64,384]{2,1,0:T(8,128)}), f32[8,64,384]{2,1,0:T(8,128)S(1)}, u32[]{:S(2)}, u32[]{:S(2)}) async-start(f32[8,64,384]{2,1,0:T(8,128)} %bitcast.25), calls=%async_computation | async-start | bytes 1572864 | tf_op jit(solution)/shard_map/all_to_all | solution.py:35
  127.1 1.2 copy-start.2
  129.2 7.4 %collective-permute-start.2 = (f32[256,768]{1,0:T(8,128)}, f32[256,768]{1,0:T(8,128)}, u32[]{:S(2)}, u32[]{:S(2)}) collective-permute-start(f32[256,768]{1,0:T(8,128)} %slice.42), channel_id=1, source_target_pairs={{0,8},{8,0},{16,24},{24,16},{32,40},{40,32},{48,56},{56,48},{64,72... | collective-permute-start | bytes 2359304 | tf_op jit(solution)/shard_map/ppermute | solution.py:46
  132.1 17.3 %all-to-all-start.4 = ((f32[8,64,384]{2,1,0:T(8,128)}), f32[8,64,384]{2,1,0:T(8,128)S(1)}, u32[]{:S(2)}, u32[]{:S(2)}) async-start(f32[8,64,384]{2,1,0:T(8,128)} %tile.5), calls=%async_computation.4 | async-start | bytes 1572864 | tf_op jit(solution)/shard_map/all_to_all | solution.py:41
  138.1 1.0 copy-start.9
  139.1 19.6 %collective-permute-start.3 = (f32[128,768]{1,0:T(8,128)}, f32[128,768]{1,0:T(8,128)}, u32[]{:S(2)}, u32[]{:S(2)}) collective-permute-start(f32[128,768]{1,0:T(8,128)} %slice.44), channel_id=1, source_target_pairs={{0,16},{8,24},{16,0},{24,8},{32,48},{40,56},{48,32},{56,40},{64,80... | collective-permute-start | bytes 1179656 | tf_op jit(solution)/shard_map/ppermute | solution.py:48
  152.1 1.2 copy-start.1
  153.2 5.5 %copy-start.10 = (f32[256,768]{1,0:T(8,128)S(1)}, f32[256,768]{1,0:T(8,128)}, u32[]{:S(2)}) copy-start(f32[256,768]{1,0:T(8,128)} %copy-done.9) | copy-start | bytes 2359300
  154.2 13.0 %collective-permute-start.6 = (f32[256,768]{1,0:T(8,128)}, f32[256,768]{1,0:T(8,128)}, u32[]{:S(2)}, u32[]{:S(2)}) collective-permute-start(f32[256,768]{1,0:T(8,128)} %slice.47), channel_id=1, source_target_pairs={{0,8},{8,0},{16,24},{24,16},{32,40},{40,32},{48,56},{56,48},{64,72... | collective-permute-start | bytes 2359304 | tf_op jit(solution)/shard_map/ppermute | solution.py:46
  160.5 31.0 %all-to-all-start.2 = ((f32[16,8,768]{2,1,0:T(8,128)}), f32[16,8,768]{2,1,0:T(8,128)}, u32[]{:S(2)}, u32[]{:S(2)}) async-start(f32[16,8,768]{2,1,0:T(8,128)} %fusion.5), calls=%async_computation.2 | async-start | bytes 786432 | tf_op jit(solution)/shard_map/all_to_all | solution.py:49
  168.7 14.2 %collective-permute-start.7 = (f32[128,768]{1,0:T(8,128)S(1)}, f32[128,768]{1,0:T(8,128)S(1)}, u32[]{:S(2)}, u32[]{:S(2)}) collective-permute-start(f32[128,768]{1,0:T(8,128)S(1)} %slice.49), channel_id=1, source_target_pairs={{0,16},{8,24},{16,0},{24,8},{32,48},{40,56},{48,32},{56,40},{64,80... | collective-permute-start | bytes 1179656 | tf_op jit(solution)/shard_map/ppermute | solution.py:48
  191.5 30.0 %all-to-all-start.5 = ((f32[16,8,768]{2,1,0:T(8,128)}), f32[16,8,768]{2,1,0:T(8,128)}, u32[]{:S(2)}, u32[]{:S(2)}) async-start(f32[16,8,768]{2,1,0:T(8,128)} %fusion.4), calls=%async_computation.5 | async-start | bytes 786432 | tf_op jit(solution)/shard_map/all_to_all | solution.py:49
  197.3 3.8 %copy-start.5 = (f32[128,768]{1,0:T(8,128)S(1)}, f32[128,768]{1,0:T(8,128)}, u32[]{:S(2)}) copy-start(f32[128,768]{1,0:T(8,128)} %copy-done.4) | copy-start | bytes 1179652
  197.3 3.8 %copy-start.8 = (f32[256,768]{1,0:T(8,128)S(1)}, f32[256,768]{1,0:T(8,128)}, u32[]{:S(2)}) copy-start(f32[256,768]{1,0:T(8,128)} %copy-done.7) | copy-start | bytes 2359300

commit v2 on v1

v2 whole, which is shorter than its diff:
```python
from functools import partial

import jax
import jax.numpy as jnp
from jax import lax
from jax.sharding import PartitionSpec as P

NZ, NY, NC = 16, 2, 2
NQ = NY * NC
Z_GROUPS = [[z * NQ + q for z in range(NZ)] for q in range(NQ)]
CORE_SWAP = [(d, d ^ 1) for d in range(NZ * NQ)]
Y_SWAP = [(d, d ^ NC) for d in range(NZ * NQ)]
BOTH_SWAP = [(d, d ^ (NC + 1)) for d in range(NZ * NQ)]

dot = partial(lax.dot_general, precision=lax.Precision.HIGH, preferred_element_type=jnp.float32)


def mm(a, b):
    return dot(a, b, (((1,), (0,)), ((), ())))


def mm_nt(a, b):
    return dot(a, b, (((1,), (1,)), ((), ())))


def mm_tn(a, b):
    return dot(a, b, (((0,), (0,)), ((), ())))


def swap(x, pairs):
    return lax.ppermute(x, "dp", pairs)


def after(x, y):
    return lax.optimization_barrier((x, y))[0]


def sum_mp(term):
    n = lax.axis_size("mp")
    got = lax.all_to_all(term, "mp", 0, 0, tiled=True)
    return got.reshape(n, term.shape[0] // n, term.shape[1]).sum(0)


def gather_mp(part):
    copies = jnp.tile(part, (lax.axis_size("mp"), 1))
    return lax.all_to_all(copies, "mp", 0, 0, tiled=True)


def shards(inputs, w_in, w_out, cotangent):
    gelu_fn = partial(jax.nn.gelu, approximate=True)
    rows, width = inputs.shape
    ff = w_in.shape[1]
    n = NZ * rows

    w_in_y = swap(w_in, Y_SWAP)
    w_out_y = swap(w_out, Y_SWAP)
    w_in_c = swap(w_in, CORE_SWAP)
    w_out_c = swap(w_out, CORE_SWAP)
    both = jnp.concatenate([inputs, cotangent], axis=0)
    ring = lax.all_gather(both, "dp", axis=0, axis_index_groups=Z_GROUPS)
    w_ins = [w_in, w_in_c, w_in_y, swap(after(w_in_y, ring), CORE_SWAP)]
    w_outs = [w_out, w_out_c, w_out_y, swap(after(w_out_y, ring), CORE_SWAP)]

    tok = ring[:, :rows].reshape(n, width)
    grd = ring[:, rows:].reshape(n, width)

    terms = jnp.concatenate([mm(tok, w) for w in w_ins] + [mm_nt(grd, w) for w in w_outs], axis=1)
    sums = sum_mp(terms)
    activated, gelu_back = jax.vjp(gelu_fn, sums[:, : NQ * ff])
    hid_grad = gelu_back(sums[:, NQ * ff :])[0]
    full = gather_mp(jnp.concatenate([activated, hid_grad], axis=1))
    act, hg = full[:, : NQ * ff], full[:, NQ * ff :]
    out_term = mm(act, jnp.concatenate(w_outs, axis=0))
    in_term = mm_nt(hg, jnp.concatenate(w_ins, axis=1))
    terms = jnp.concatenate([out_term.reshape(NZ, rows, width), in_term.reshape(NZ, rows, width)], axis=1)
    got = lax.all_to_all(terms, "dp", 0, 0, tiled=True, axis_index_groups=Z_GROUPS).sum(0)
    output, input_grad = got[:rows], got[rows:]

    tg = jnp.concatenate([tok, grd], axis=0)
    tg_y = swap(after(tg, full), Y_SWAP)
    part = [jnp.concatenate([act[:, k * ff : (k + 1) * ff], hg[:, k * ff : (k + 1) * ff]], axis=1) for k in range(NQ)]
    part_y = swap(part[2], Y_SWAP)
    part_yc = swap(part[3], BOTH_SWAP)
    part_c = swap(part[1], CORE_SWAP)
    tg_c = swap(tg, CORE_SWAP)
    tg_yc = swap(tg_y, CORE_SWAP)

    def grads(tgs, parts):
        t = jnp.concatenate([x[:n] for x in tgs], axis=0)
        c = jnp.concatenate([x[n:] for x in tgs], axis=0)
        p = jnp.concatenate(parts, axis=0)
        return mm_tn(t, p[:, ff:]), mm_tn(p[:, :ff], c)

    near, far = grads([tg, tg_c], [part[0], part_c]), grads([tg_y, tg_yc], [part_y, part_yc])
    w_in_grad = near[0] + far[0]
    w_out_grad = near[1] + far[1]
    return (output, input_grad, w_in_grad, w_out_grad)


def solution(mesh):
    placed = (P("dp", "mp"), P("mp", "dp"), P("dp", "mp"), P("dp", "mp"))
    return jax.shard_map(
        shards,
        mesh=mesh,
        in_specs=placed,
        out_specs=(P("dp", "mp"), P("dp", "mp"), P("mp", "dp"), P("dp", "mp")),
        check_vma=False,
    )
```

time: 224 us -> 186 us (0.83)
  the two profiles are of different devices: /device:TPU:2 before, /device:TPU:32 now
where the time goes in v2:
time: 186 us
  blocking collectives  65.1 us (35%)
  starting transfers between devices  52.7 us (28%)
  waiting for transfers between devices  39.9 us (21%)
  matrix products  17.2 us (9%)
  local copies, waits for them, and re-layouts  6.6 us (4%)
  other arithmetic  3.05 us (2%)
    all_gather x1, blocking collectives, shards(): ring = lax.all_gather(both, 'dp', axis=0, axis_index_groups=Z_GROUPS)  38 us
    ppermute x12, starting transfers between devices, swap(): return lax.ppermute(x, 'dp', pairs)  34 us
    all_to_all x1, blocking collectives, sum_mp(): got = lax.all_to_all(term, 'mp', 0, 0, tiled=True)  27.1 us
    all_to_all x1, waiting for transfers between devices, gather_mp(): return lax.all_to_all(copies, 'mp', 0, 0, tiled=True)  18.5 us
    all_to_all x1, starting transfers between devices, shards(): lax.all_to_all(terms, 'dp', 0, 0, tiled=True, axis_index_groups=Z_GROUPS)  15.2 us
    all_to_all x1, waiting for transfers between devices, shards(): lax.all_to_all(terms, 'dp', 0, 0, tiled=True, axis_index_groups=Z_GROUPS)  12.2 us
    ppermute x12, waiting for transfers between devices, swap(): return lax.ppermute(x, 'dp', pairs)  9.17 us
    dot_general x5, matrix products, mm_nt(): return dot(a, b, (((1,), (1,)), ((), ())))  6.7 us
  transfers between devices with their start and end apart: 14, of which 5 were waited for; matrix products, arithmetic and copies ran while one was open for 12% of the time, Pallas kernels for 0%

profile of v2, /device:TPU:32, one launch (start us, length us, event | category | flops | bytes accessed | tf_op | source)
XLA Modules:
  0.0 185.6 jit_solution(13871158140489593562)
XLA Ops:
  0.6 5.1 %collective-permute-start.1 = (f32[768,384]{1,0:T(8,128)}, f32[768,384]{1,0:T(8,128)S(1)}, u32[]{:S(2)}, u32[]{:S(2)}) collective-permute-start(f32[768,384]{1,0:T(8,128)} %param.5), channel_id=1, source_target_pairs={{0,16},{8,24},{16,0},{24,8},{32,48},{40,56},{48,32},{56,40},{64,80... | collective-permute-start | bytes 3538952 | tf_op jit(solution)/shard_map/ppermute | solution.py:31
  5.7 2.2 %collective-permute-start.4 = (f32[384,768]{1,0:T(8,128)}, f32[384,768]{1,0:T(8,128)S(1)}, u32[]{:S(2)}, u32[]{:S(2)}) collective-permute-start(f32[384,768]{1,0:T(8,128)} %param.6), channel_id=1, source_target_pairs={{0,16},{8,24},{16,0},{24,8},{32,48},{40,56},{48,32},{56,40},{64,80... | collective-permute-start | bytes 3538952 | tf_op jit(solution)/shard_map/ppermute | solution.py:31
  8.0 1.9 %collective-permute-start = (f32[768,384]{1,0:T(8,128)}, f32[768,384]{1,0:T(8,128)S(1)}, u32[]{:S(2)}, u32[]{:S(2)}) collective-permute-start(f32[768,384]{1,0:T(8,128)} %param.5), channel_id=1, source_target_pairs={{0,8},{8,0},{16,24},{24,16},{32,40},{40,32},{48,56},{56,48},{64,72... | collective-permute-start | bytes 3538952 | tf_op jit(solution)/shard_map/ppermute | solution.py:31
  10.7 38.0 %all-gather = f32[256,768]{1,0:T(8,128)S(1)} all-gather(f32[16,768]{1,0:T(8,128)S(1)} %pad_maximum_fusion.9), channel_id=2, replica_groups={{0,32,64,96,128,160,192,224,256,288,320,352,384,416,448,480},{8,40,72,1..., dimensions={0}, use_global_device_ids=true | all-gather | bytes 835584 | tf_op jit(solution)/shard_map/all_gather | solution.py:60
  48.7 1.9 %collective-permute-start.2 = (f32[768,384]{1,0:T(8,128)S(1)}, f32[768,384]{1,0:T(8,128)S(1)}, u32[]{:S(2)}, u32[]{:S(2)}) collective-permute-start(f32[768,384]{1,0:T(8,128)S(1)} %collective-permute-done.1), channel_id=1, source_target_pairs={{0,8},{8,0},{16,24},{24,16},{32,40},{40,32},{48,56},{56,48},{64,72... | collective-permute-start | bytes 3538952 | tf_op jit(solution)/shard_map/ppermute | solution.py:31
  50.6 2.4 %collective-permute-start.3 = (f32[384,768]{1,0:T(8,128)}, f32[384,768]{1,0:T(8,128)S(1)}, u32[]{:S(2)}, u32[]{:S(2)}) collective-permute-start(f32[384,768]{1,0:T(8,128)} %param.6), channel_id=1, source_target_pairs={{0,8},{8,0},{16,24},{24,16},{32,40},{40,32},{48,56},{56,48},{64,72... | collective-permute-start | bytes 3538952 | tf_op jit(solution)/shard_map/ppermute | solution.py:31
  54.8 2.4 %collective-permute-done.4 = f32[384,768]{1,0:T(8,128)S(1)} collective-permute-done((f32[384,768]{1,0:T(8,128)}, f32[384,768]{1,0:T(8,128)S(1)}, u32[]{:S(2)}, u32[]{:S(2)}) %collective-permute-start.4) | collective-permute-done | bytes 1179680 | tf_op jit(solution)/shard_map/ppermute | solution.py:31
  57.2 1.9 %collective-permute-start.5 = (f32[384,768]{1,0:T(8,128)S(1)}, f32[384,768]{1,0:T(8,128)S(1)}, u32[]{:S(2)}, u32[]{:S(2)}) collective-permute-start(f32[384,768]{1,0:T(8,128)S(1)} %collective-permute-done.4), channel_id=1, source_target_pairs={{0,8},{8,0},{16,24},{24,16},{32,40},{40,32},{48,56},{56,48},{64,72... | collective-permute-start | bytes 3538952 | tf_op jit(solution)/shard_map/ppermute | solution.py:31
  65.6 27.1 %all_to_all.23 = f32[8,16,3072]{2,1,0:T(8,128)S(1)} all-to-all(f32[8,16,3072]{2,1,0:T(8,128)S(1)} %bitcast.39), channel_id=1, replica_groups=mesh['dp'=64,'mp'=8] {'mp'}, dimensions={0} | all-to-all | bytes 3145728 | tf_op jit(solution)/shard_map/all_to_all | solution.py:40
  94.2 3.6 %all-to-all-start.1 = ((f32[8,16,3072]{2,1,0:T(8,128)}), f32[8,16,3072]{2,1,0:T(8,128)S(1)}, u32[]{:S(2)}, u32[]{:S(2)}) async-start(f32[8,16,3072]{2,1,0:T(8,128)} %tile.2), calls=%async_computation.1 | async-start | bytes 3145728 | tf_op jit(solution)/shard_map/all_to_all | solution.py:46
  98.8 1.9 %collective-permute-start.6 = (f32[256,768]{1,0:T(8,128)}, f32[256,768]{1,0:T(8,128)}, u32[]{:S(2)}, u32[]{:S(2)}) collective-permute-start(f32[256,768]{1,0:T(8,128)} %pad_maximum_fusion), channel_id=1, source_target_pairs={{0,8},{8,0},{16,24},{24,16},{32,40},{40,32},{48,56},{56,48},{64,72... | collective-permute-start | bytes 2359304 | tf_op jit(solution)/shard_map/ppermute | solution.py:31
  100.7 18.5 %all-to-all-done.1 = f32[8,16,3072]{2,1,0:T(8,128)S(1)} async-done(((f32[8,16,3072]{2,1,0:T(8,128)}), f32[8,16,3072]{2,1,0:T(8,128)S(1)}, u32[]{:S(2)}, u32[]{:S(2)}) %all-to-all-start.1) | async-done | bytes 1572896 | tf_op jit(solution)/shard_map/all_to_all | solution.py:46
  119.2 5.1 %collective-permute-start.8 = (f32[256,768]{1,0:T(8,128)}, f32[256,768]{1,0:T(8,128)}, u32[]{:S(2)}, u32[]{:S(2)}) collective-permute-start(f32[256,768]{1,0:T(8,128)} %pad_maximum_fusion), channel_id=1, source_target_pairs={{0,16},{8,24},{16,0},{24,8},{32,48},{40,56},{48,32},{56,40},{64,80... | collective-permute-start | bytes 2359304 | tf_op jit(solution)/shard_map/ppermute | solution.py:31
  124.2 4.0 %fusion.16 = f32[16,8,768]{2,1,0:T(8,128)S(1)} fusion(f32[768,384]{1,0:T(8,128)} %copy-done.6, f32[768,384]{1,0:T(8,128)} %copy-done.2, f32[768,384]{1,0:T(8,128)} %copy-done.5, f32[768,384]{1,0:T(8,128)} %param.5, f32[128,3072]{1,0:T(8,128)S(1)} %bitcast.36), kind=kOutput, calls=%fused_computation.18 | convolution fusion | flops 909508608 | bytes 5898240 | tf_op jit(solution)/shard_map/dot_general | solution.py:23
  128.3 2.1 %fusion.19 = f32[16,8,768]{2,1,0:T(8,128)S(1)} fusion(f32[384,768]{1,0:T(8,128)S(1)} %copy-done.10, f32[384,768]{1,0:T(8,128)S(1)} %copy-done.4, f32[384,768]{1,0:T(8,128)S(1)} %copy-done.8, f32[384,768]{1,0:T(8,128)S(1)} %copy-done.1, f32[128,3072]{1,0:T(8,128)S(1)} %bitcast.37), kind=kOutput, calls=%fused_computation.19 | convolution fusion | flops 909508608 | bytes 5898240 | tf_op jit(solution)/shard_map/dot_general | solution.py:19
  131.4 15.2 %all-to-all-start.2 = ((f32[16,16,768]{2,1,0:T(8,128)}), f32[16,16,768]{2,1,0:T(8,128)S(1)}, u32[]{:S(2)}, u32[]{:S(2)}) async-start(f32[16,16,768]{2,1,0:T(8,128)} %pad_maximum_fusion.3), calls=%async_computation.2 | async-start | bytes 1572864 | tf_op jit(solution)/shard_map/all_to_all | solution.py:76
  146.7 2.5 %collective-permute-start.10 = (f32[128,768]{1,0:T(8,128)S(1)}, f32[128,768]{1,0:T(8,128)S(1)}, u32[]{:S(2)}, u32[]{:S(2)}) collective-permute-start(f32[128,768]{1,0:T(8,128)S(1)} %pad_maximum_fusion.6), channel_id=1, source_target_pairs={{0,16},{8,24},{16,0},{24,8},{32,48},{40,56},{48,32},{56,40},{64,80... | collective-permute-start | bytes 1179656 | tf_op jit(solution)/shard_map/ppermute | solution.py:31
  149.3 3.0 %collective-permute-start.11 = (f32[128,768]{1,0:T(8,128)S(1)}, f32[128,768]{1,0:T(8,128)S(1)}, u32[]{:S(2)}, u32[]{:S(2)}) collective-permute-start(f32[128,768]{1,0:T(8,128)S(1)} %pad_maximum_fusion.7), channel_id=1, source_target_pairs={{0,24},{8,16},{16,8},{24,0},{32,56},{40,48},{48,40},{56,32},{64,88... | collective-permute-start | bytes 1179656 | tf_op jit(solution)/shard_map/ppermute | solution.py:31
  152.4 3.8 %collective-permute-start.7 = (f32[128,768]{1,0:T(8,128)S(1)}, f32[128,768]{1,0:T(8,128)S(1)}, u32[]{:S(2)}, u32[]{:S(2)}) collective-permute-start(f32[128,768]{1,0:T(8,128)S(1)} %pad_maximum_fusion.5), channel_id=1, source_target_pairs={{0,8},{8,0},{16,24},{24,16},{32,40},{40,32},{48,56},{56,48},{64,72... | collective-permute-start | bytes 1179656 | tf_op jit(solution)/shard_map/ppermute | solution.py:31
  156.2 2.1 %collective-permute-start.9 = (f32[256,768]{1,0:T(8,128)}, f32[256,768]{1,0:T(8,128)S(1)}, u32[]{:S(2)}, u32[]{:S(2)}) collective-permute-start(f32[256,768]{1,0:T(8,128)} %collective-permute-done.8), channel_id=1, source_target_pairs={{0,8},{8,0},{16,24},{24,16},{32,40},{40,32},{48,56},{56,48},{64,72... | collective-permute-start | bytes 2359304 | tf_op jit(solution)/shard_map/ppermute | solution.py:31
  159.5 2.7 %collective-permute-done.10 = f32[128,768]{1,0:T(8,128)S(1)} collective-permute-done((f32[128,768]{1,0:T(8,128)S(1)}, f32[128,768]{1,0:T(8,128)S(1)}, u32[]{:S(2)}, u32[]{:S(2)}) %collective-permute-start.10) | collective-permute-done | bytes 393248 | tf_op jit(solution)/shard_map/ppermute | solution.py:31
  162.2 4.0 %collective-permute-done.11 = f32[128,768]{1,0:T(8,128)S(1)} collective-permute-done((f32[128,768]{1,0:T(8,128)S(1)}, f32[128,768]{1,0:T(8,128)S(1)}, u32[]{:S(2)}, u32[]{:S(2)}) %collective-permute-start.11) | collective-permute-done | bytes 393248 | tf_op jit(solution)/shard_map/ppermute | solution.py:31
  169.2 1.8 convolution_add_fusion.1
  172.7 12.2 %all-to-all-done.2 = f32[16,16,768]{2,1,0:T(8,128)S(1)} async-done(((f32[16,16,768]{2,1,0:T(8,128)}), f32[16,16,768]{2,1,0:T(8,128)S(1)}, u32[]{:S(2)}, u32[]{:S(2)}) %all-to-all-start.2) | async-done | bytes 786464 | tf_op jit(solution)/shard_map/all_to_all | solution.py:76
  (62 shorter events, 18.9 us)
Async XLA Ops:
  0.6 48.1 %collective-permute-start.1 = (f32[768,384]{1,0:T(8,128)}, f32[768,384]{1,0:T(8,128)S(1)}, u32[]{:S(2)}, u32[]{:S(2)}) collective-permute-start(f32[768,384]{1,0:T(8,128)} %param.5), channel_id=1, source_target_pairs={{0,16},{8,24},{16,0},{24,8},{32,48},{40,56},{48,32},{56,40},{64,80... | collective-permute-start | bytes 3538952 | tf_op jit(solution)/shard_map/ppermute | solution.py:31
  5.7 51.5 %collective-permute-start.4 = (f32[384,768]{1,0:T(8,128)}, f32[384,768]{1,0:T(8,128)S(1)}, u32[]{:S(2)}, u32[]{:S(2)}) collective-permute-start(f32[384,768]{1,0:T(8,128)} %param.6), channel_id=1, source_target_pairs={{0,16},{8,24},{16,0},{24,8},{32,48},{40,56},{48,32},{56,40},{64,80... | collective-permute-start | bytes 3538952 | tf_op jit(solution)/shard_map/ppermute | solution.py:31
  8.0 51.2 %collective-permute-start = (f32[768,384]{1,0:T(8,128)}, f32[768,384]{1,0:T(8,128)S(1)}, u32[]{:S(2)}, u32[]{:S(2)}) collective-permute-start(f32[768,384]{1,0:T(8,128)} %param.5), channel_id=1, source_target_pairs={{0,8},{8,0},{16,24},{24,16},{32,40},{40,32},{48,56},{56,48},{64,72... | collective-permute-start | bytes 3538952 | tf_op jit(solution)/shard_map/ppermute | solution.py:31
  48.7 11.0 %copy-start.2 = (f32[768,384]{1,0:T(8,128)}, f32[768,384]{1,0:T(8,128)S(1)}, u32[]{:S(2)}) copy-start(f32[768,384]{1,0:T(8,128)S(1)} %collective-permute-done.1) | copy-start | bytes 3538948
  48.7 12.0 %collective-permute-start.2 = (f32[768,384]{1,0:T(8,128)S(1)}, f32[768,384]{1,0:T(8,128)S(1)}, u32[]{:S(2)}, u32[]{:S(2)}) collective-permute-start(f32[768,384]{1,0:T(8,128)S(1)} %collective-permute-done.1), channel_id=1, source_target_pairs={{0,8},{8,0},{16,24},{24,16},{32,40},{40,32},{48,56},{56,48},{64,72... | collective-permute-start | bytes 3538952 | tf_op jit(solution)/shard_map/ppermute | solution.py:31
  50.6 12.5 %collective-permute-start.3 = (f32[384,768]{1,0:T(8,128)}, f32[384,768]{1,0:T(8,128)S(1)}, u32[]{:S(2)}, u32[]{:S(2)}) collective-permute-start(f32[384,768]{1,0:T(8,128)} %param.6), channel_id=1, source_target_pairs={{0,8},{8,0},{16,24},{24,16},{32,40},{40,32},{48,56},{56,48},{64,72... | collective-permute-start | bytes 3538952 | tf_op jit(solution)/shard_map/ppermute | solution.py:31
  57.2 6.6 %copy-start.3 = (f32[384,768]{1,0:T(8,128)}, f32[384,768]{1,0:T(8,128)S(1)}, u32[]{:S(2)}) copy-start(f32[384,768]{1,0:T(8,128)S(1)} %collective-permute-done.4) | copy-start | bytes 3538948
  57.2 7.3 %collective-permute-start.5 = (f32[384,768]{1,0:T(8,128)S(1)}, f32[384,768]{1,0:T(8,128)S(1)}, u32[]{:S(2)}, u32[]{:S(2)}) collective-permute-start(f32[384,768]{1,0:T(8,128)S(1)} %collective-permute-done.4), channel_id=1, source_target_pairs={{0,8},{8,0},{16,24},{24,16},{32,40},{40,32},{48,56},{56,48},{64,72... | collective-permute-start | bytes 3538952 | tf_op jit(solution)/shard_map/ppermute | solution.py:31
  59.2 1.0 copy-start.5
  60.7 1.7 copy-start
  60.7 2.4 %copy-start.6 = (f32[768,384]{1,0:T(8,128)}, f32[768,384]{1,0:T(8,128)S(1)}, u32[]{:S(2)}) copy-start(f32[768,384]{1,0:T(8,128)S(1)} %collective-permute-done.2) | copy-start | bytes 3538948
  63.1 1.4 copy-start.7
  94.2 25.0 %all-to-all-start.1 = ((f32[8,16,3072]{2,1,0:T(8,128)}), f32[8,16,3072]{2,1,0:T(8,128)S(1)}, u32[]{:S(2)}, u32[]{:S(2)}) async-start(f32[8,16,3072]{2,1,0:T(8,128)} %tile.2), calls=%async_computation.1 | async-start | bytes 3145728 | tf_op jit(solution)/shard_map/all_to_all | solution.py:46
  98.8 59.6 %collective-permute-start.6 = (f32[256,768]{1,0:T(8,128)}, f32[256,768]{1,0:T(8,128)}, u32[]{:S(2)}, u32[]{:S(2)}) collective-permute-start(f32[256,768]{1,0:T(8,128)} %pad_maximum_fusion), channel_id=1, source_target_pairs={{0,8},{8,0},{16,24},{24,16},{32,40},{40,32},{48,56},{56,48},{64,72... | collective-permute-start | bytes 2359304 | tf_op jit(solution)/shard_map/ppermute | solution.py:31
  119.2 9.1 %copy-start.1 = (f32[384,768]{1,0:T(8,128)S(1)}, f32[384,768]{1,0:T(8,128)}, u32[]{:S(2)}) copy-start(f32[384,768]{1,0:T(8,128)} %param.6) | copy-start | bytes 3538948
  119.2 9.1 %copy-start.4 = (f32[384,768]{1,0:T(8,128)S(1)}, f32[384,768]{1,0:T(8,128)}, u32[]{:S(2)}) copy-start(f32[384,768]{1,0:T(8,128)} %copy-done.3) | copy-start | bytes 3538948
  119.2 9.1 %copy-start.8 = (f32[384,768]{1,0:T(8,128)S(1)}, f32[384,768]{1,0:T(8,128)}, u32[]{:S(2)}) copy-start(f32[384,768]{1,0:T(8,128)} %copy-done.7) | copy-start | bytes 3538948
  119.2 9.1 %copy-start.10 = (f32[384,768]{1,0:T(8,128)S(1)}, f32[384,768]{1,0:T(8,128)}, u32[]{:S(2)}) copy-start(f32[384,768]{1,0:T(8,128)} %copy-done.9) | copy-start | bytes 3538948
  119.2 37.1 %collective-permute-start.8 = (f32[256,768]{1,0:T(8,128)}, f32[256,768]{1,0:T(8,128)}, u32[]{:S(2)}, u32[]{:S(2)}) collective-permute-start(f32[256,768]{1,0:T(8,128)} %pad_maximum_fusion), channel_id=1, source_target_pairs={{0,16},{8,24},{16,0},{24,8},{32,48},{40,56},{48,32},{56,40},{64,80... | collective-permute-start | bytes 2359304 | tf_op jit(solution)/shard_map/ppermute | solution.py:31
  131.4 53.6 %all-to-all-start.2 = ((f32[16,16,768]{2,1,0:T(8,128)}), f32[16,16,768]{2,1,0:T(8,128)S(1)}, u32[]{:S(2)}, u32[]{:S(2)}) async-start(f32[16,16,768]{2,1,0:T(8,128)} %pad_maximum_fusion.3), calls=%async_computation.2 | async-start | bytes 1572864 | tf_op jit(solution)/shard_map/all_to_all | solution.py:76
  146.7 15.5 %collective-permute-start.10 = (f32[128,768]{1,0:T(8,128)S(1)}, f32[128,768]{1,0:T(8,128)S(1)}, u32[]{:S(2)}, u32[]{:S(2)}) collective-permute-start(f32[128,768]{1,0:T(8,128)S(1)} %pad_maximum_fusion.6), channel_id=1, source_target_pairs={{0,16},{8,24},{16,0},{24,8},{32,48},{40,56},{48,32},{56,40},{64,80... | collective-permute-start | bytes 1179656 | tf_op jit(solution)/shard_map/ppermute | solution.py:31
  149.3 16.9 %collective-permute-start.11 = (f32[128,768]{1,0:T(8,128)S(1)}, f32[128,768]{1,0:T(8,128)S(1)}, u32[]{:S(2)}, u32[]{:S(2)}) collective-permute-start(f32[128,768]{1,0:T(8,128)S(1)} %pad_maximum_fusion.7), channel_id=1, source_target_pairs={{0,24},{8,16},{16,8},{24,0},{32,56},{40,48},{48,40},{56,32},{64,88... | collective-permute-start | bytes 1179656 | tf_op jit(solution)/shard_map/ppermute | solution.py:31
  152.4 13.9 %collective-permute-start.7 = (f32[128,768]{1,0:T(8,128)S(1)}, f32[128,768]{1,0:T(8,128)S(1)}, u32[]{:S(2)}, u32[]{:S(2)}) collective-permute-start(f32[128,768]{1,0:T(8,128)S(1)} %pad_maximum_fusion.5), channel_id=1, source_target_pairs={{0,8},{8,0},{16,24},{24,16},{32,40},{40,32},{48,56},{56,48},{64,72... | collective-permute-start | bytes 1179656 | tf_op jit(solution)/shard_map/ppermute | solution.py:31
  156.2 11.3 %collective-permute-start.9 = (f32[256,768]{1,0:T(8,128)}, f32[256,768]{1,0:T(8,128)S(1)}, u32[]{:S(2)}, u32[]{:S(2)}) collective-permute-start(f32[256,768]{1,0:T(8,128)} %collective-permute-done.8), channel_id=1, source_target_pairs={{0,8},{8,0},{16,24},{24,16},{32,40},{40,32},{48,56},{56,48},{64,72... | collective-permute-start | bytes 2359304 | tf_op jit(solution)/shard_map/ppermute | solution.py:31
  (1 other events, 1.0 us)

commit v3 on v2

--- a/solution.py
+++ b/solution.py
@@ -77,12 +77,12 @@
     output, input_grad = got[:rows], got[rows:]
 
     tg = jnp.concatenate([tok, grd], axis=0)
-    tg_y = swap(after(tg, full), Y_SWAP)
+    tg_c = swap(after(tg, sums), CORE_SWAP)
+    tg_y = swap(after(tg, tg_c), Y_SWAP)
     part = [jnp.concatenate([act[:, k * ff : (k + 1) * ff], hg[:, k * ff : (k + 1) * ff]], axis=1) for k in range(NQ)]
     part_y = swap(part[2], Y_SWAP)
     part_yc = swap(part[3], BOTH_SWAP)
     part_c = swap(part[1], CORE_SWAP)
-    tg_c = swap(tg, CORE_SWAP)
     tg_yc = swap(tg_y, CORE_SWAP)
 
     def grads(tgs, parts):

time: 186 us -> 182 us (0.978)
  waiting for transfers between devices: 39.9 us -> 34.7 us
    all_to_all x1, waiting for transfers between devices: 18.5 us -> 10.4 us  [gather_mp(): return lax.all_to_all(copies, 'mp', 0, 0, tiled=True)]
    ppermute x12, waiting for transfers between devices: 9.17 us -> 13.8 us  [swap(): return lax.ppermute(x, 'dp', pairs)]
  transfers between devices with their start and end apart: 14 -> 14, of which waited for: 5 -> 6; matrix products, arithmetic and copies ran while one was open for 12% -> 12% of each run, Pallas kernels for 0% -> 0%
where the time goes in v3:
time: 182 us; the launch traced here: 181 us
  blocking collectives  65.1 us (36%)
  starting transfers between devices  52.5 us (29%)
  waiting for transfers between devices  34.7 us (19%)
  matrix products  17.3 us (10%)
  local copies, waits for them, and re-layouts  7.54 us (4%)
  other arithmetic  3.01 us (2%)
    all_gather x1, blocking collectives, shards(): ring = lax.all_gather(both, 'dp', axis=0, axis_index_groups=Z_GROUPS)  38 us
    ppermute x12, starting transfers between devices, swap(): return lax.ppermute(x, 'dp', pairs)  33.7 us
    all_to_all x1, blocking collectives, sum_mp(): got = lax.all_to_all(term, 'mp', 0, 0, tiled=True)  27.1 us
    all_to_all x1, starting transfers between devices, shards(): lax.all_to_all(terms, 'dp', 0, 0, tiled=True, axis_index_groups=Z_GROUPS)  15.2 us
    ppermute x12, waiting for transfers between devices, swap(): return lax.ppermute(x, 'dp', pairs)  13.8 us
    all_to_all x1, waiting for transfers between devices, shards(): lax.all_to_all(terms, 'dp', 0, 0, tiled=True, axis_index_groups=Z_GROUPS)  10.5 us
    all_to_all x1, waiting for transfers between devices, gather_mp(): return lax.all_to_all(copies, 'mp', 0, 0, tiled=True)  10.4 us
    dot_general x5, matrix products, mm_nt(): return dot(a, b, (((1,), (1,)), ((), ())))  6.84 us
  transfers between devices with their start and end apart: 14, of which 6 were waited for; matrix products, arithmetic and copies ran while one was open for 12% of the time, Pallas kernels for 0%

profile of v3, /device:TPU:32, one launch (start us, length us, event | category | flops | bytes accessed | tf_op | source)
XLA Modules:
  0.0 181.2 jit_solution(16927090434102011501)
XLA Ops:
  0.6 5.1 %collective-permute-start.1 = (f32[768,384]{1,0:T(8,128)}, f32[768,384]{1,0:T(8,128)S(1)}, u32[]{:S(2)}, u32[]{:S(2)}) collective-permute-start(f32[768,384]{1,0:T(8,128)} %param.5), channel_id=1, source_target_pairs={{0,16},{8,24},{16,0},{24,8},{32,48},{40,56},{48,32},{56,40},{64,80... | collective-permute-start | bytes 3538952 | tf_op jit(solution)/shard_map/ppermute | solution.py:31
  5.7 2.2 %collective-permute-start.4 = (f32[384,768]{1,0:T(8,128)}, f32[384,768]{1,0:T(8,128)S(1)}, u32[]{:S(2)}, u32[]{:S(2)}) collective-permute-start(f32[384,768]{1,0:T(8,128)} %param.6), channel_id=1, source_target_pairs={{0,16},{8,24},{16,0},{24,8},{32,48},{40,56},{48,32},{56,40},{64,80... | collective-permute-start | bytes 3538952 | tf_op jit(solution)/shard_map/ppermute | solution.py:31
  8.0 1.9 %collective-permute-start = (f32[768,384]{1,0:T(8,128)}, f32[768,384]{1,0:T(8,128)S(1)}, u32[]{:S(2)}, u32[]{:S(2)}) collective-permute-start(f32[768,384]{1,0:T(8,128)} %param.5), channel_id=1, source_target_pairs={{0,8},{8,0},{16,24},{24,16},{32,40},{40,32},{48,56},{56,48},{64,72... | collective-permute-start | bytes 3538952 | tf_op jit(solution)/shard_map/ppermute | solution.py:31
  10.7 38.0 %all-gather = f32[256,768]{1,0:T(8,128)S(1)} all-gather(f32[16,768]{1,0:T(8,128)S(1)} %pad_maximum_fusion.9), channel_id=2, replica_groups={{0,32,64,96,128,160,192,224,256,288,320,352,384,416,448,480},{8,40,72,1..., dimensions={0}, use_global_device_ids=true | all-gather | bytes 835584 | tf_op jit(solution)/shard_map/all_gather | solution.py:60
  48.7 1.9 %collective-permute-start.2 = (f32[768,384]{1,0:T(8,128)S(1)}, f32[768,384]{1,0:T(8,128)S(1)}, u32[]{:S(2)}, u32[]{:S(2)}) collective-permute-start(f32[768,384]{1,0:T(8,128)S(1)} %collective-permute-done.1), channel_id=1, source_target_pairs={{0,8},{8,0},{16,24},{24,16},{32,40},{40,32},{48,56},{56,48},{64,72... | collective-permute-start | bytes 3538952 | tf_op jit(solution)/shard_map/ppermute | solution.py:31
  50.6 2.4 %collective-permute-start.3 = (f32[384,768]{1,0:T(8,128)}, f32[384,768]{1,0:T(8,128)S(1)}, u32[]{:S(2)}, u32[]{:S(2)}) collective-permute-start(f32[384,768]{1,0:T(8,128)} %param.6), channel_id=1, source_target_pairs={{0,8},{8,0},{16,24},{24,16},{32,40},{40,32},{48,56},{56,48},{64,72... | collective-permute-start | bytes 3538952 | tf_op jit(solution)/shard_map/ppermute | solution.py:31
  54.8 2.4 %collective-permute-done.4 = f32[384,768]{1,0:T(8,128)S(1)} collective-permute-done((f32[384,768]{1,0:T(8,128)}, f32[384,768]{1,0:T(8,128)S(1)}, u32[]{:S(2)}, u32[]{:S(2)}) %collective-permute-start.4) | collective-permute-done | bytes 1179680 | tf_op jit(solution)/shard_map/ppermute | solution.py:31
  57.2 1.9 %collective-permute-start.5 = (f32[384,768]{1,0:T(8,128)S(1)}, f32[384,768]{1,0:T(8,128)S(1)}, u32[]{:S(2)}, u32[]{:S(2)}) collective-permute-start(f32[384,768]{1,0:T(8,128)S(1)} %collective-permute-done.4), channel_id=1, source_target_pairs={{0,8},{8,0},{16,24},{24,16},{32,40},{40,32},{48,56},{56,48},{64,72... | collective-permute-start | bytes 3538952 | tf_op jit(solution)/shard_map/ppermute | solution.py:31
  65.5 27.1 %all_to_all.23 = f32[8,16,3072]{2,1,0:T(8,128)S(1)} all-to-all(f32[8,16,3072]{2,1,0:T(8,128)S(1)} %bitcast.39), channel_id=1, replica_groups=mesh['dp'=64,'mp'=8] {'mp'}, dimensions={0} | all-to-all | bytes 3145728 | tf_op jit(solution)/shard_map/all_to_all | solution.py:40
  94.2 3.6 %all-to-all-start.1 = ((f32[8,16,3072]{2,1,0:T(8,128)}), f32[8,16,3072]{2,1,0:T(8,128)S(1)}, u32[]{:S(2)}, u32[]{:S(2)}) async-start(f32[8,16,3072]{2,1,0:T(8,128)} %tile.2), calls=%async_computation.1 | async-start | bytes 3145728 | tf_op jit(solution)/shard_map/all_to_all | solution.py:46
  98.8 1.9 %collective-permute-start.6 = (f32[256,768]{1,0:T(8,128)}, f32[256,768]{1,0:T(8,128)S(1)}, u32[]{:S(2)}, u32[]{:S(2)}) collective-permute-start(f32[256,768]{1,0:T(8,128)} %pad_maximum_fusion), channel_id=1, source_target_pairs={{0,8},{8,0},{16,24},{24,16},{32,40},{40,32},{48,56},{56,48},{64,72... | collective-permute-start | bytes 2359304 | tf_op jit(solution)/shard_map/ppermute | solution.py:31
  100.7 2.5 %collective-permute-done.6 = f32[256,768]{1,0:T(8,128)S(1)} collective-permute-done((f32[256,768]{1,0:T(8,128)}, f32[256,768]{1,0:T(8,128)S(1)}, u32[]{:S(2)}, u32[]{:S(2)}) %collective-permute-start.6) | collective-permute-done | bytes 786464 | tf_op jit(solution)/shard_map/ppermute | solution.py:31
  104.1 4.8 %collective-permute-start.8 = (f32[256,768]{1,0:T(8,128)}, f32[256,768]{1,0:T(8,128)}, u32[]{:S(2)}, u32[]{:S(2)}) collective-permute-start(f32[256,768]{1,0:T(8,128)} %pad_maximum_fusion), channel_id=1, source_target_pairs={{0,16},{8,24},{16,0},{24,8},{32,48},{40,56},{48,32},{56,40},{64,80... | collective-permute-start | bytes 2359304 | tf_op jit(solution)/shard_map/ppermute | solution.py:31
  108.9 10.4 %all-to-all-done.1 = f32[8,16,3072]{2,1,0:T(8,128)S(1)} async-done(((f32[8,16,3072]{2,1,0:T(8,128)}), f32[8,16,3072]{2,1,0:T(8,128)S(1)}, u32[]{:S(2)}, u32[]{:S(2)}) %all-to-all-start.1) | async-done | bytes 1572896 | tf_op jit(solution)/shard_map/all_to_all | solution.py:46
  119.3 4.2 %fusion.16 = f32[16,8,768]{2,1,0:T(8,128)S(1)} fusion(f32[768,384]{1,0:T(8,128)} %copy-done.6, f32[768,384]{1,0:T(8,128)} %copy-done.2, f32[768,384]{1,0:T(8,128)} %copy-done.5, f32[768,384]{1,0:T(8,128)} %param.5, f32[128,3072]{1,0:T(8,128)S(1)} %bitcast.36), kind=kOutput, calls=%fused_computation.18 | convolution fusion | flops 909508608 | bytes 5898240 | tf_op jit(solution)/shard_map/dot_general | solution.py:23
  123.5 2.1 %fusion.19 = f32[16,8,768]{2,1,0:T(8,128)S(1)} fusion(f32[384,768]{1,0:T(8,128)S(1)} %copy-done.10, f32[384,768]{1,0:T(8,128)S(1)} %copy-done.4, f32[384,768]{1,0:T(8,128)S(1)} %copy-done.8, f32[384,768]{1,0:T(8,128)S(1)} %copy-done.1, f32[128,3072]{1,0:T(8,128)S(1)} %bitcast.37), kind=kOutput, calls=%fused_computation.19 | convolution fusion | flops 909508608 | bytes 5898240 | tf_op jit(solution)/shard_map/dot_general | solution.py:19
  126.5 15.2 %all-to-all-start.2 = ((f32[16,16,768]{2,1,0:T(8,128)}), f32[16,16,768]{2,1,0:T(8,128)S(1)}, u32[]{:S(2)}, u32[]{:S(2)}) async-start(f32[16,16,768]{2,1,0:T(8,128)} %pad_maximum_fusion.3), calls=%async_computation.2 | async-start | bytes 1572864 | tf_op jit(solution)/shard_map/all_to_all | solution.py:76
  143.1 4.8 %collective-permute-start.10 = (f32[128,768]{1,0:T(8,128)S(1)}, f32[128,768]{1,0:T(8,128)S(1)}, u32[]{:S(2)}, u32[]{:S(2)}) collective-permute-start(f32[128,768]{1,0:T(8,128)S(1)} %pad_maximum_fusion.6), channel_id=1, source_target_pairs={{0,16},{8,24},{16,0},{24,8},{32,48},{40,56},{48,32},{56,40},{64,80... | collective-permute-start | bytes 1179656 | tf_op jit(solution)/shard_map/ppermute | solution.py:31
  147.9 1.9 %collective-permute-start.9 = (f32[256,768]{1,0:T(8,128)}, f32[256,768]{1,0:T(8,128)S(1)}, u32[]{:S(2)}, u32[]{:S(2)}) collective-permute-start(f32[256,768]{1,0:T(8,128)} %collective-permute-done.8), channel_id=1, source_target_pairs={{0,8},{8,0},{16,24},{24,16},{32,40},{40,32},{48,56},{56,48},{64,72... | collective-permute-start | bytes 2359304 | tf_op jit(solution)/shard_map/ppermute | solution.py:31
  149.8 2.6 %collective-permute-start.11 = (f32[128,768]{1,0:T(8,128)S(1)}, f32[128,768]{1,0:T(8,128)S(1)}, u32[]{:S(2)}, u32[]{:S(2)}) collective-permute-start(f32[128,768]{1,0:T(8,128)S(1)} %pad_maximum_fusion.7), channel_id=1, source_target_pairs={{0,24},{8,16},{16,8},{24,0},{32,56},{40,48},{48,40},{56,32},{64,88... | collective-permute-start | bytes 1179656 | tf_op jit(solution)/shard_map/ppermute | solution.py:31
  152.5 2.1 %collective-permute-start.7 = (f32[128,768]{1,0:T(8,128)S(1)}, f32[128,768]{1,0:T(8,128)S(1)}, u32[]{:S(2)}, u32[]{:S(2)}) collective-permute-start(f32[128,768]{1,0:T(8,128)S(1)} %pad_maximum_fusion.5), channel_id=1, source_target_pairs={{0,8},{8,0},{16,24},{24,16},{32,40},{40,32},{48,56},{56,48},{64,72... | collective-permute-start | bytes 1179656 | tf_op jit(solution)/shard_map/ppermute | solution.py:31
  157.5 7.3 %collective-permute-done.11 = f32[128,768]{1,0:T(8,128)S(1)} collective-permute-done((f32[128,768]{1,0:T(8,128)S(1)}, f32[128,768]{1,0:T(8,128)S(1)}, u32[]{:S(2)}, u32[]{:S(2)}) %collective-permute-start.11) | collective-permute-done | bytes 393248 | tf_op jit(solution)/shard_map/ppermute | solution.py:31
  166.4 1.8 %convolution_add_fusion.1 = f32[768,384]{1,0:T(8,128)} fusion(f32[768,384]{1,0:T(8,128)S(1)} %fusion.25, f32[128,768]{1,0:T(8,128)S(1)} %get-tuple-element.27, f32[128,768]{1,0:T(8,128)S(1)} %get-tuple-element.21, f32[256,768]{1,0:T(8,128)S(1)} %pad_maximum_fusion.4), kind=kOutput, calls=%fused_computation.17 | convolution fusion | flops 453476352 | bytes 3538944 | tf_op jit(solution)/shard_map/dot_general | solution.py:27
  170.0 10.5 %all-to-all-done.2 = f32[16,16,768]{2,1,0:T(8,128)S(1)} async-done(((f32[16,16,768]{2,1,0:T(8,128)}), f32[16,16,768]{2,1,0:T(8,128)S(1)}, u32[]{:S(2)}, u32[]{:S(2)}) %all-to-all-start.2) | async-done | bytes 786464 | tf_op jit(solution)/shard_map/all_to_all | solution.py:76
  (64 shorter events, 21.4 us)
Async XLA Ops:
  0.6 48.1 %collective-permute-start.1 = (f32[768,384]{1,0:T(8,128)}, f32[768,384]{1,0:T(8,128)S(1)}, u32[]{:S(2)}, u32[]{:S(2)}) collective-permute-start(f32[768,384]{1,0:T(8,128)} %param.5), channel_id=1, source_target_pairs={{0,16},{8,24},{16,0},{24,8},{32,48},{40,56},{48,32},{56,40},{64,80... | collective-permute-start | bytes 3538952 | tf_op jit(solution)/shard_map/ppermute | solution.py:31
  5.7 51.5 %collective-permute-start.4 = (f32[384,768]{1,0:T(8,128)}, f32[384,768]{1,0:T(8,128)S(1)}, u32[]{:S(2)}, u32[]{:S(2)}) collective-permute-start(f32[384,768]{1,0:T(8,128)} %param.6), channel_id=1, source_target_pairs={{0,16},{8,24},{16,0},{24,8},{32,48},{40,56},{48,32},{56,40},{64,80... | collective-permute-start | bytes 3538952 | tf_op jit(solution)/shard_map/ppermute | solution.py:31
  8.0 51.2 %collective-permute-start = (f32[768,384]{1,0:T(8,128)}, f32[768,384]{1,0:T(8,128)S(1)}, u32[]{:S(2)}, u32[]{:S(2)}) collective-permute-start(f32[768,384]{1,0:T(8,128)} %param.5), channel_id=1, source_target_pairs={{0,8},{8,0},{16,24},{24,16},{32,40},{40,32},{48,56},{56,48},{64,72... | collective-permute-start | bytes 3538952 | tf_op jit(solution)/shard_map/ppermute | solution.py:31
  48.7 11.0 %copy-start.2 = (f32[768,384]{1,0:T(8,128)}, f32[768,384]{1,0:T(8,128)S(1)}, u32[]{:S(2)}) copy-start(f32[768,384]{1,0:T(8,128)S(1)} %collective-permute-done.1) | copy-start | bytes 3538948
  48.7 12.0 %collective-permute-start.2 = (f32[768,384]{1,0:T(8,128)S(1)}, f32[768,384]{1,0:T(8,128)S(1)}, u32[]{:S(2)}, u32[]{:S(2)}) collective-permute-start(f32[768,384]{1,0:T(8,128)S(1)} %collective-permute-done.1), channel_id=1, source_target_pairs={{0,8},{8,0},{16,24},{24,16},{32,40},{40,32},{48,56},{56,48},{64,72... | collective-permute-start | bytes 3538952 | tf_op jit(solution)/shard_map/ppermute | solution.py:31
  50.6 12.5 %collective-permute-start.3 = (f32[384,768]{1,0:T(8,128)}, f32[384,768]{1,0:T(8,128)S(1)}, u32[]{:S(2)}, u32[]{:S(2)}) collective-permute-start(f32[384,768]{1,0:T(8,128)} %param.6), channel_id=1, source_target_pairs={{0,8},{8,0},{16,24},{24,16},{32,40},{40,32},{48,56},{56,48},{64,72... | collective-permute-start | bytes 3538952 | tf_op jit(solution)/shard_map/ppermute | solution.py:31
  57.2 6.6 %copy-start.3 = (f32[384,768]{1,0:T(8,128)}, f32[384,768]{1,0:T(8,128)S(1)}, u32[]{:S(2)}) copy-start(f32[384,768]{1,0:T(8,128)S(1)} %collective-permute-done.4) | copy-start | bytes 3538948
  57.2 7.3 %collective-permute-start.5 = (f32[384,768]{1,0:T(8,128)S(1)}, f32[384,768]{1,0:T(8,128)S(1)}, u32[]{:S(2)}, u32[]{:S(2)}) collective-permute-start(f32[384,768]{1,0:T(8,128)S(1)} %collective-permute-done.4), channel_id=1, source_target_pairs={{0,8},{8,0},{16,24},{24,16},{32,40},{40,32},{48,56},{56,48},{64,72... | collective-permute-start | bytes 3538952 | tf_op jit(solution)/shard_map/ppermute | solution.py:31
  59.2 1.0 copy-start.5
  60.7 1.7 copy-start
  60.7 2.4 %copy-start.6 = (f32[768,384]{1,0:T(8,128)}, f32[768,384]{1,0:T(8,128)S(1)}, u32[]{:S(2)}) copy-start(f32[768,384]{1,0:T(8,128)S(1)} %collective-permute-done.2) | copy-start | bytes 3538948
  63.1 1.4 copy-start.7
  94.2 25.1 %all-to-all-start.1 = ((f32[8,16,3072]{2,1,0:T(8,128)}), f32[8,16,3072]{2,1,0:T(8,128)S(1)}, u32[]{:S(2)}, u32[]{:S(2)}) async-start(f32[8,16,3072]{2,1,0:T(8,128)} %tile.2), calls=%async_computation.1 | async-start | bytes 3145728 | tf_op jit(solution)/shard_map/all_to_all | solution.py:46
  98.8 4.4 %collective-permute-start.6 = (f32[256,768]{1,0:T(8,128)}, f32[256,768]{1,0:T(8,128)S(1)}, u32[]{:S(2)}, u32[]{:S(2)}) collective-permute-start(f32[256,768]{1,0:T(8,128)} %pad_maximum_fusion), channel_id=1, source_target_pairs={{0,8},{8,0},{16,24},{24,16},{32,40},{40,32},{48,56},{56,48},{64,72... | collective-permute-start | bytes 2359304 | tf_op jit(solution)/shard_map/ppermute | solution.py:31
  104.1 43.8 %collective-permute-start.8 = (f32[256,768]{1,0:T(8,128)}, f32[256,768]{1,0:T(8,128)}, u32[]{:S(2)}, u32[]{:S(2)}) collective-permute-start(f32[256,768]{1,0:T(8,128)} %pad_maximum_fusion), channel_id=1, source_target_pairs={{0,16},{8,24},{16,0},{24,8},{32,48},{40,56},{48,32},{56,40},{64,80... | collective-permute-start | bytes 2359304 | tf_op jit(solution)/shard_map/ppermute | solution.py:31
  119.3 4.2 %copy-start.1 = (f32[384,768]{1,0:T(8,128)S(1)}, f32[384,768]{1,0:T(8,128)}, u32[]{:S(2)}) copy-start(f32[384,768]{1,0:T(8,128)} %param.6) | copy-start | bytes 3538948
  119.3 4.2 %copy-start.4 = (f32[384,768]{1,0:T(8,128)S(1)}, f32[384,768]{1,0:T(8,128)}, u32[]{:S(2)}) copy-start(f32[384,768]{1,0:T(8,128)} %copy-done.3) | copy-start | bytes 3538948
  119.3 4.2 %copy-start.8 = (f32[384,768]{1,0:T(8,128)S(1)}, f32[384,768]{1,0:T(8,128)}, u32[]{:S(2)}) copy-start(f32[384,768]{1,0:T(8,128)} %copy-done.7) | copy-start | bytes 3538948
  119.3 4.2 %copy-start.10 = (f32[384,768]{1,0:T(8,128)S(1)}, f32[384,768]{1,0:T(8,128)}, u32[]{:S(2)}) copy-start(f32[384,768]{1,0:T(8,128)} %copy-done.9) | copy-start | bytes 3538948
  126.5 54.0 %all-to-all-start.2 = ((f32[16,16,768]{2,1,0:T(8,128)}), f32[16,16,768]{2,1,0:T(8,128)S(1)}, u32[]{:S(2)}, u32[]{:S(2)}) async-start(f32[16,16,768]{2,1,0:T(8,128)} %pad_maximum_fusion.3), calls=%async_computation.2 | async-start | bytes 1572864 | tf_op jit(solution)/shard_map/all_to_all | solution.py:76
  143.1 14.4 %collective-permute-start.10 = (f32[128,768]{1,0:T(8,128)S(1)}, f32[128,768]{1,0:T(8,128)S(1)}, u32[]{:S(2)}, u32[]{:S(2)}) collective-permute-start(f32[128,768]{1,0:T(8,128)S(1)} %pad_maximum_fusion.6), channel_id=1, source_target_pairs={{0,16},{8,24},{16,0},{24,8},{32,48},{40,56},{48,32},{56,40},{64,80... | collective-permute-start | bytes 1179656 | tf_op jit(solution)/shard_map/ppermute | solution.py:31
  147.9 16.9 %collective-permute-start.9 = (f32[256,768]{1,0:T(8,128)}, f32[256,768]{1,0:T(8,128)S(1)}, u32[]{:S(2)}, u32[]{:S(2)}) collective-permute-start(f32[256,768]{1,0:T(8,128)} %collective-permute-done.8), channel_id=1, source_target_pairs={{0,8},{8,0},{16,24},{24,16},{32,40},{40,32},{48,56},{56,48},{64,72... | collective-permute-start | bytes 2359304 | tf_op jit(solution)/shard_map/ppermute | solution.py:31
  149.8 14.9 %collective-permute-start.11 = (f32[128,768]{1,0:T(8,128)S(1)}, f32[128,768]{1,0:T(8,128)S(1)}, u32[]{:S(2)}, u32[]{:S(2)}) collective-permute-start(f32[128,768]{1,0:T(8,128)S(1)} %pad_maximum_fusion.7), channel_id=1, source_target_pairs={{0,24},{8,16},{16,8},{24,0},{32,56},{40,48},{48,40},{56,32},{64,88... | collective-permute-start | bytes 1179656 | tf_op jit(solution)/shard_map/ppermute | solution.py:31
  152.5 12.2 %collective-permute-start.7 = (f32[128,768]{1,0:T(8,128)S(1)}, f32[128,768]{1,0:T(8,128)S(1)}, u32[]{:S(2)}, u32[]{:S(2)}) collective-permute-start(f32[128,768]{1,0:T(8,128)S(1)} %pad_maximum_fusion.5), channel_id=1, source_target_pairs={{0,8},{8,0},{16,24},{24,16},{32,40},{40,32},{48,56},{56,48},{64,72... | collective-permute-start | bytes 1179656 | tf_op jit(solution)/shard_map/ppermute | solution.py:31
  (2 other events, 2.0 us)

commit v4 on v3

--- a/solution.py
+++ b/solution.py
@@ -59,12 +59,13 @@
     both = jnp.concatenate([inputs, cotangent], axis=0)
     ring = lax.all_gather(both, "dp", axis=0, axis_index_groups=Z_GROUPS)
     w_ins = [w_in, w_in_c, w_in_y, swap(after(w_in_y, ring), CORE_SWAP)]
-    w_outs = [w_out, w_out_c, w_out_y, swap(after(w_out_y, ring), CORE_SWAP)]
-
     tok = ring[:, :rows].reshape(n, width)
     grd = ring[:, rows:].reshape(n, width)
 
-    terms = jnp.concatenate([mm(tok, w) for w in w_ins] + [mm_nt(grd, w) for w in w_outs], axis=1)
+    blocks = [mm(tok, w_in), mm(tok, w_in_c), mm_nt(grd, w_out), mm_nt(grd, w_out_c)]
+    w_outs = [w_out, w_out_c, w_out_y, swap(after(w_out_y, blocks[:2]), CORE_SWAP)]
+    terms = blocks[:2] + [mm(tok, w) for w in w_ins[2:]] + blocks[2:] + [mm_nt(grd, w) for w in w_outs[2:]]
+    terms = jnp.concatenate(terms, axis=1)
     sums = sum_mp(terms)
     activated, gelu_back = jax.vjp(gelu_fn, sums[:, : NQ * ff])
     hid_grad = gelu_back(sums[:, NQ * ff :])[0]

time: 182 us -> 181 us (level)
  no operation moved by 1% of the time
where the time goes in v4:
time: 181 us; the launch traced here: 180 us
  blocking collectives  65 us (36%)
  starting transfers between devices  52.5 us (29%)
  waiting for transfers between devices  34.2 us (19%)
  matrix products  17.3 us (10%)
  local copies, waits for them, and re-layouts  7.04 us (4%)
  other arithmetic  3.01 us (2%)
    all_gather x1, blocking collectives, shards(): ring = lax.all_gather(both, 'dp', axis=0, axis_index_groups=Z_GROUPS)  37.9 us
    ppermute x12, starting transfers between devices, swap(): return lax.ppermute(x, 'dp', pairs)  33.7 us
    all_to_all x1, blocking collectives, sum_mp(): got = lax.all_to_all(term, 'mp', 0, 0, tiled=True)  27.1 us
    all_to_all x1, starting transfers between devices, shards(): lax.all_to_all(terms, 'dp', 0, 0, tiled=True, axis_index_groups=Z_GROUPS)  15.2 us
    ppermute x12, waiting for transfers between devices, swap(): return lax.ppermute(x, 'dp', pairs)  13.3 us
    all_to_all x1, waiting for transfers between devices, shards(): lax.all_to_all(terms, 'dp', 0, 0, tiled=True, axis_index_groups=Z_GROUPS)  10.5 us
    all_to_all x1, waiting for transfers between devices, gather_mp(): return lax.all_to_all(copies, 'mp', 0, 0, tiled=True)  10.4 us
    dot_general x5, matrix products, mm_nt(): return dot(a, b, (((1,), (1,)), ((), ())))  6.85 us
  transfers between devices with their start and end apart: 14, of which 6 were waited for; matrix products, arithmetic and copies ran while one was open for 12% of the time, Pallas kernels for 0%

profile of v4, /device:TPU:32, one launch (start us, length us, event | category | flops | bytes accessed | tf_op | source)
XLA Modules:
  0.0 180.2 jit_solution(8269654689473882904)
XLA Ops:
  0.6 5.1 %collective-permute-start.1 = (f32[768,384]{1,0:T(8,128)}, f32[768,384]{1,0:T(8,128)S(1)}, u32[]{:S(2)}, u32[]{:S(2)}) collective-permute-start(f32[768,384]{1,0:T(8,128)} %param.5), channel_id=1, source_target_pairs={{0,16},{8,24},{16,0},{24,8},{32,48},{40,56},{48,32},{56,40},{64,80... | collective-permute-start | bytes 3538952 | tf_op jit(solution)/shard_map/ppermute | solution.py:31
  5.7 1.9 %collective-permute-start = (f32[768,384]{1,0:T(8,128)}, f32[768,384]{1,0:T(8,128)S(1)}, u32[]{:S(2)}, u32[]{:S(2)}) collective-permute-start(f32[768,384]{1,0:T(8,128)} %param.5), channel_id=1, source_target_pairs={{0,8},{8,0},{16,24},{24,16},{32,40},{40,32},{48,56},{56,48},{64,72... | collective-permute-start | bytes 3538952 | tf_op jit(solution)/shard_map/ppermute | solution.py:31
  7.7 2.2 %collective-permute-start.4 = (f32[384,768]{1,0:T(8,128)}, f32[384,768]{1,0:T(8,128)S(1)}, u32[]{:S(2)}, u32[]{:S(2)}) collective-permute-start(f32[384,768]{1,0:T(8,128)} %param.6), channel_id=1, source_target_pairs={{0,16},{8,24},{16,0},{24,8},{32,48},{40,56},{48,32},{56,40},{64,80... | collective-permute-start | bytes 3538952 | tf_op jit(solution)/shard_map/ppermute | solution.py:31
  10.7 37.9 %all-gather = f32[256,768]{1,0:T(8,128)S(1)} all-gather(f32[16,768]{1,0:T(8,128)S(1)} %pad_maximum_fusion.9), channel_id=2, replica_groups={{0,32,64,96,128,160,192,224,256,288,320,352,384,416,448,480},{8,40,72,1..., dimensions={0}, use_global_device_ids=true | all-gather | bytes 835584 | tf_op jit(solution)/shard_map/all_gather | solution.py:60
  48.6 1.9 %collective-permute-start.2 = (f32[768,384]{1,0:T(8,128)S(1)}, f32[768,384]{1,0:T(8,128)S(1)}, u32[]{:S(2)}, u32[]{:S(2)}) collective-permute-start(f32[768,384]{1,0:T(8,128)S(1)} %collective-permute-done.1), channel_id=1, source_target_pairs={{0,8},{8,0},{16,24},{24,16},{32,40},{40,32},{48,56},{56,48},{64,72... | collective-permute-start | bytes 3538952 | tf_op jit(solution)/shard_map/ppermute | solution.py:31
  50.6 2.4 %collective-permute-start.3 = (f32[384,768]{1,0:T(8,128)}, f32[384,768]{1,0:T(8,128)S(1)}, u32[]{:S(2)}, u32[]{:S(2)}) collective-permute-start(f32[384,768]{1,0:T(8,128)} %param.6), channel_id=1, source_target_pairs={{0,8},{8,0},{16,24},{24,16},{32,40},{40,32},{48,56},{56,48},{64,72... | collective-permute-start | bytes 3538952 | tf_op jit(solution)/shard_map/ppermute | solution.py:31
  55.3 1.9 %collective-permute-done.4 = f32[384,768]{1,0:T(8,128)S(1)} collective-permute-done((f32[384,768]{1,0:T(8,128)}, f32[384,768]{1,0:T(8,128)S(1)}, u32[]{:S(2)}, u32[]{:S(2)}) %collective-permute-start.4) | collective-permute-done | bytes 1179680 | tf_op jit(solution)/shard_map/ppermute | solution.py:31
  57.2 1.9 %collective-permute-start.5 = (f32[384,768]{1,0:T(8,128)S(1)}, f32[384,768]{1,0:T(8,128)S(1)}, u32[]{:S(2)}, u32[]{:S(2)}) collective-permute-start(f32[384,768]{1,0:T(8,128)S(1)} %collective-permute-done.4), channel_id=1, source_target_pairs={{0,8},{8,0},{16,24},{24,16},{32,40},{40,32},{48,56},{56,48},{64,72... | collective-permute-start | bytes 3538952 | tf_op jit(solution)/shard_map/ppermute | solution.py:31
  64.5 27.1 %all_to_all.23 = f32[8,16,3072]{2,1,0:T(8,128)S(1)} all-to-all(f32[8,16,3072]{2,1,0:T(8,128)S(1)} %bitcast.43), channel_id=1, replica_groups=mesh['dp'=64,'mp'=8] {'mp'}, dimensions={0} | all-to-all | bytes 3145728 | tf_op jit(solution)/shard_map/all_to_all | solution.py:40
  93.1 3.6 %all-to-all-start.1 = ((f32[8,16,3072]{2,1,0:T(8,128)}), f32[8,16,3072]{2,1,0:T(8,128)S(1)}, u32[]{:S(2)}, u32[]{:S(2)}) async-start(f32[8,16,3072]{2,1,0:T(8,128)} %tile.2), calls=%async_computation.1 | async-start | bytes 3145728 | tf_op jit(solution)/shard_map/all_to_all | solution.py:46
  97.7 1.9 %collective-permute-start.6 = (f32[256,768]{1,0:T(8,128)}, f32[256,768]{1,0:T(8,128)S(1)}, u32[]{:S(2)}, u32[]{:S(2)}) collective-permute-start(f32[256,768]{1,0:T(8,128)} %pad_maximum_fusion), channel_id=1, source_target_pairs={{0,8},{8,0},{16,24},{24,16},{32,40},{40,32},{48,56},{56,48},{64,72... | collective-permute-start | bytes 2359304 | tf_op jit(solution)/shard_map/ppermute | solution.py:31
  99.6 2.5 %collective-permute-done.6 = f32[256,768]{1,0:T(8,128)S(1)} collective-permute-done((f32[256,768]{1,0:T(8,128)}, f32[256,768]{1,0:T(8,128)S(1)}, u32[]{:S(2)}, u32[]{:S(2)}) %collective-permute-start.6) | collective-permute-done | bytes 786464 | tf_op jit(solution)/shard_map/ppermute | solution.py:31
  103.0 4.8 %collective-permute-start.8 = (f32[256,768]{1,0:T(8,128)}, f32[256,768]{1,0:T(8,128)}, u32[]{:S(2)}, u32[]{:S(2)}) collective-permute-start(f32[256,768]{1,0:T(8,128)} %pad_maximum_fusion), channel_id=1, source_target_pairs={{0,16},{8,24},{16,0},{24,8},{32,48},{40,56},{48,32},{56,40},{64,80... | collective-permute-start | bytes 2359304 | tf_op jit(solution)/shard_map/ppermute | solution.py:31
  107.8 10.4 %all-to-all-done.1 = f32[8,16,3072]{2,1,0:T(8,128)S(1)} async-done(((f32[8,16,3072]{2,1,0:T(8,128)}), f32[8,16,3072]{2,1,0:T(8,128)S(1)}, u32[]{:S(2)}, u32[]{:S(2)}) %all-to-all-start.1) | async-done | bytes 1572896 | tf_op jit(solution)/shard_map/all_to_all | solution.py:46
  118.2 4.2 %fusion.16 = f32[16,8,768]{2,1,0:T(8,128)S(1)} fusion(f32[768,384]{1,0:T(8,128)} %copy-done.6, f32[768,384]{1,0:T(8,128)} %copy-done.2, f32[768,384]{1,0:T(8,128)} %copy-done.3, f32[768,384]{1,0:T(8,128)} %param.5, f32[128,3072]{1,0:T(8,128)S(1)} %bitcast.40), kind=kOutput, calls=%fused_computation.18 | convolution fusion | flops 909508608 | bytes 5898240 | tf_op jit(solution)/shard_map/dot_general | solution.py:23
  122.5 2.1 %fusion.19 = f32[16,8,768]{2,1,0:T(8,128)S(1)} fusion(f32[384,768]{1,0:T(8,128)S(1)} %copy-done.10, f32[384,768]{1,0:T(8,128)S(1)} %copy-done.5, f32[384,768]{1,0:T(8,128)S(1)} %copy-done.8, f32[384,768]{1,0:T(8,128)S(1)} %copy-done.1, f32[128,3072]{1,0:T(8,128)S(1)} %bitcast.41), kind=kOutput, calls=%fused_computation.19 | convolution fusion | flops 909508608 | bytes 5898240 | tf_op jit(solution)/shard_map/dot_general | solution.py:19
  125.5 15.2 %all-to-all-start.2 = ((f32[16,16,768]{2,1,0:T(8,128)}), f32[16,16,768]{2,1,0:T(8,128)S(1)}, u32[]{:S(2)}, u32[]{:S(2)}) async-start(f32[16,16,768]{2,1,0:T(8,128)} %pad_maximum_fusion.3), calls=%async_computation.2 | async-start | bytes 1572864 | tf_op jit(solution)/shard_map/all_to_all | solution.py:77
  142.0 4.8 %collective-permute-start.10 = (f32[128,768]{1,0:T(8,128)S(1)}, f32[128,768]{1,0:T(8,128)S(1)}, u32[]{:S(2)}, u32[]{:S(2)}) collective-permute-start(f32[128,768]{1,0:T(8,128)S(1)} %pad_maximum_fusion.6), channel_id=1, source_target_pairs={{0,16},{8,24},{16,0},{24,8},{32,48},{40,56},{48,32},{56,40},{64,80... | collective-permute-start | bytes 1179656 | tf_op jit(solution)/shard_map/ppermute | solution.py:31
  146.9 1.9 %collective-permute-start.9 = (f32[256,768]{1,0:T(8,128)}, f32[256,768]{1,0:T(8,128)S(1)}, u32[]{:S(2)}, u32[]{:S(2)}) collective-permute-start(f32[256,768]{1,0:T(8,128)} %collective-permute-done.8), channel_id=1, source_target_pairs={{0,8},{8,0},{16,24},{24,16},{32,40},{40,32},{48,56},{56,48},{64,72... | collective-permute-start | bytes 2359304 | tf_op jit(solution)/shard_map/ppermute | solution.py:31
  148.8 2.6 %collective-permute-start.11 = (f32[128,768]{1,0:T(8,128)S(1)}, f32[128,768]{1,0:T(8,128)S(1)}, u32[]{:S(2)}, u32[]{:S(2)}) collective-permute-start(f32[128,768]{1,0:T(8,128)S(1)} %pad_maximum_fusion.7), channel_id=1, source_target_pairs={{0,24},{8,16},{16,8},{24,0},{32,56},{40,48},{48,40},{56,32},{64,88... | collective-permute-start | bytes 1179656 | tf_op jit(solution)/shard_map/ppermute | solution.py:31
  151.5 2.1 %collective-permute-start.7 = (f32[128,768]{1,0:T(8,128)S(1)}, f32[128,768]{1,0:T(8,128)S(1)}, u32[]{:S(2)}, u32[]{:S(2)}) collective-permute-start(f32[128,768]{1,0:T(8,128)S(1)} %pad_maximum_fusion.5), channel_id=1, source_target_pairs={{0,8},{8,0},{16,24},{24,16},{32,40},{40,32},{48,56},{56,48},{64,72... | collective-permute-start | bytes 1179656 | tf_op jit(solution)/shard_map/ppermute | solution.py:31
  156.4 7.3 %collective-permute-done.11 = f32[128,768]{1,0:T(8,128)S(1)} collective-permute-done((f32[128,768]{1,0:T(8,128)S(1)}, f32[128,768]{1,0:T(8,128)S(1)}, u32[]{:S(2)}, u32[]{:S(2)}) %collective-permute-start.11) | collective-permute-done | bytes 393248 | tf_op jit(solution)/shard_map/ppermute | solution.py:31
  165.4 1.8 %convolution_add_fusion.1 = f32[768,384]{1,0:T(8,128)} fusion(f32[768,384]{1,0:T(8,128)S(1)} %fusion.25, f32[128,768]{1,0:T(8,128)S(1)} %get-tuple-element.27, f32[128,768]{1,0:T(8,128)S(1)} %get-tuple-element.21, f32[256,768]{1,0:T(8,128)S(1)} %pad_maximum_fusion.4), kind=kOutput, calls=%fused_computation.17 | convolution fusion | flops 453476352 | bytes 3538944 | tf_op jit(solution)/shard_map/dot_general | solution.py:27
  169.0 10.5 %all-to-all-done.2 = f32[16,16,768]{2,1,0:T(8,128)S(1)} async-done(((f32[16,16,768]{2,1,0:T(8,128)}), f32[16,16,768]{2,1,0:T(8,128)S(1)}, u32[]{:S(2)}, u32[]{:S(2)}) %all-to-all-start.2) | async-done | bytes 786464 | tf_op jit(solution)/shard_map/all_to_all | solution.py:77
  (64 shorter events, 20.9 us)
Async XLA Ops:
  0.6 48.0 %collective-permute-start.1 = (f32[768,384]{1,0:T(8,128)}, f32[768,384]{1,0:T(8,128)S(1)}, u32[]{:S(2)}, u32[]{:S(2)}) collective-permute-start(f32[768,384]{1,0:T(8,128)} %param.5), channel_id=1, source_target_pairs={{0,16},{8,24},{16,0},{24,8},{32,48},{40,56},{48,32},{56,40},{64,80... | collective-permute-start | bytes 3538952 | tf_op jit(solution)/shard_map/ppermute | solution.py:31
  5.7 49.0 %collective-permute-start = (f32[768,384]{1,0:T(8,128)}, f32[768,384]{1,0:T(8,128)S(1)}, u32[]{:S(2)}, u32[]{:S(2)}) collective-permute-start(f32[768,384]{1,0:T(8,128)} %param.5), channel_id=1, source_target_pairs={{0,8},{8,0},{16,24},{24,16},{32,40},{40,32},{48,56},{56,48},{64,72... | collective-permute-start | bytes 3538952 | tf_op jit(solution)/shard_map/ppermute | solution.py:31
  7.7 49.6 %collective-permute-start.4 = (f32[384,768]{1,0:T(8,128)}, f32[384,768]{1,0:T(8,128)S(1)}, u32[]{:S(2)}, u32[]{:S(2)}) collective-permute-start(f32[384,768]{1,0:T(8,128)} %param.6), channel_id=1, source_target_pairs={{0,16},{8,24},{16,0},{24,8},{32,48},{40,56},{48,32},{56,40},{64,80... | collective-permute-start | bytes 3538952 | tf_op jit(solution)/shard_map/ppermute | solution.py:31
  48.6 10.5 %copy-start.2 = (f32[768,384]{1,0:T(8,128)}, f32[768,384]{1,0:T(8,128)S(1)}, u32[]{:S(2)}) copy-start(f32[768,384]{1,0:T(8,128)S(1)} %collective-permute-done.1) | copy-start | bytes 3538948
  48.6 11.1 %collective-permute-start.2 = (f32[768,384]{1,0:T(8,128)S(1)}, f32[768,384]{1,0:T(8,128)S(1)}, u32[]{:S(2)}, u32[]{:S(2)}) collective-permute-start(f32[768,384]{1,0:T(8,128)S(1)} %collective-permute-done.1), channel_id=1, source_target_pairs={{0,8},{8,0},{16,24},{24,16},{32,40},{40,32},{48,56},{56,48},{64,72... | collective-permute-start | bytes 3538952 | tf_op jit(solution)/shard_map/ppermute | solution.py:31
  50.6 11.5 %collective-permute-start.3 = (f32[384,768]{1,0:T(8,128)}, f32[384,768]{1,0:T(8,128)S(1)}, u32[]{:S(2)}, u32[]{:S(2)}) collective-permute-start(f32[384,768]{1,0:T(8,128)} %param.6), channel_id=1, source_target_pairs={{0,8},{8,0},{16,24},{24,16},{32,40},{40,32},{48,56},{56,48},{64,72... | collective-permute-start | bytes 3538952 | tf_op jit(solution)/shard_map/ppermute | solution.py:31
  54.8 4.4 %copy-start.3 = (f32[768,384]{1,0:T(8,128)}, f32[768,384]{1,0:T(8,128)S(1)}, u32[]{:S(2)}) copy-start(f32[768,384]{1,0:T(8,128)S(1)} %collective-permute-done) | copy-start | bytes 3538948
  57.2 5.5 %copy-start.4 = (f32[384,768]{1,0:T(8,128)}, f32[384,768]{1,0:T(8,128)S(1)}, u32[]{:S(2)}) copy-start(f32[384,768]{1,0:T(8,128)S(1)} %collective-permute-done.4) | copy-start | bytes 3538948
  57.2 6.2 %collective-permute-start.5 = (f32[384,768]{1,0:T(8,128)S(1)}, f32[384,768]{1,0:T(8,128)S(1)}, u32[]{:S(2)}, u32[]{:S(2)}) collective-permute-start(f32[384,768]{1,0:T(8,128)S(1)} %collective-permute-done.4), channel_id=1, source_target_pairs={{0,8},{8,0},{16,24},{24,16},{32,40},{40,32},{48,56},{56,48},{64,72... | collective-permute-start | bytes 3538952 | tf_op jit(solution)/shard_map/ppermute | solution.py:31
  59.7 1.7 copy-start
  59.7 2.4 %copy-start.6 = (f32[768,384]{1,0:T(8,128)}, f32[768,384]{1,0:T(8,128)S(1)}, u32[]{:S(2)}) copy-start(f32[768,384]{1,0:T(8,128)S(1)} %collective-permute-done.2) | copy-start | bytes 3538948
  62.1 1.4 copy-start.7
  93.1 25.1 %all-to-all-start.1 = ((f32[8,16,3072]{2,1,0:T(8,128)}), f32[8,16,3072]{2,1,0:T(8,128)S(1)}, u32[]{:S(2)}, u32[]{:S(2)}) async-start(f32[8,16,3072]{2,1,0:T(8,128)} %tile.2), calls=%async_computation.1 | async-start | bytes 3145728 | tf_op jit(solution)/shard_map/all_to_all | solution.py:46
  97.7 4.4 %collective-permute-start.6 = (f32[256,768]{1,0:T(8,128)}, f32[256,768]{1,0:T(8,128)S(1)}, u32[]{:S(2)}, u32[]{:S(2)}) collective-permute-start(f32[256,768]{1,0:T(8,128)} %pad_maximum_fusion), channel_id=1, source_target_pairs={{0,8},{8,0},{16,24},{24,16},{32,40},{40,32},{48,56},{56,48},{64,72... | collective-permute-start | bytes 2359304 | tf_op jit(solution)/shard_map/ppermute | solution.py:31
  103.0 43.8 %collective-permute-start.8 = (f32[256,768]{1,0:T(8,128)}, f32[256,768]{1,0:T(8,128)}, u32[]{:S(2)}, u32[]{:S(2)}) collective-permute-start(f32[256,768]{1,0:T(8,128)} %pad_maximum_fusion), channel_id=1, source_target_pairs={{0,16},{8,24},{16,0},{24,8},{32,48},{40,56},{48,32},{56,40},{64,80... | collective-permute-start | bytes 2359304 | tf_op jit(solution)/shard_map/ppermute | solution.py:31
  118.2 4.2 %copy-start.1 = (f32[384,768]{1,0:T(8,128)S(1)}, f32[384,768]{1,0:T(8,128)}, u32[]{:S(2)}) copy-start(f32[384,768]{1,0:T(8,128)} %param.6) | copy-start | bytes 3538948
  118.2 4.2 %copy-start.5 = (f32[384,768]{1,0:T(8,128)S(1)}, f32[384,768]{1,0:T(8,128)}, u32[]{:S(2)}) copy-start(f32[384,768]{1,0:T(8,128)} %copy-done.4) | copy-start | bytes 3538948
  118.2 4.2 %copy-start.8 = (f32[384,768]{1,0:T(8,128)S(1)}, f32[384,768]{1,0:T(8,128)}, u32[]{:S(2)}) copy-start(f32[384,768]{1,0:T(8,128)} %copy-done.7) | copy-start | bytes 3538948
  118.2 4.2 %copy-start.10 = (f32[384,768]{1,0:T(8,128)S(1)}, f32[384,768]{1,0:T(8,128)}, u32[]{:S(2)}) copy-start(f32[384,768]{1,0:T(8,128)} %copy-done.9) | copy-start | bytes 3538948
  125.5 54.0 %all-to-all-start.2 = ((f32[16,16,768]{2,1,0:T(8,128)}), f32[16,16,768]{2,1,0:T(8,128)S(1)}, u32[]{:S(2)}, u32[]{:S(2)}) async-start(f32[16,16,768]{2,1,0:T(8,128)} %pad_maximum_fusion.3), calls=%async_computation.2 | async-start | bytes 1572864 | tf_op jit(solution)/shard_map/all_to_all | solution.py:77
  142.0 14.4 %collective-permute-start.10 = (f32[128,768]{1,0:T(8,128)S(1)}, f32[128,768]{1,0:T(8,128)S(1)}, u32[]{:S(2)}, u32[]{:S(2)}) collective-permute-start(f32[128,768]{1,0:T(8,128)S(1)} %pad_maximum_fusion.6), channel_id=1, source_target_pairs={{0,16},{8,24},{16,0},{24,8},{32,48},{40,56},{48,32},{56,40},{64,80... | collective-permute-start | bytes 1179656 | tf_op jit(solution)/shard_map/ppermute | solution.py:31
  146.9 16.9 %collective-permute-start.9 = (f32[256,768]{1,0:T(8,128)}, f32[256,768]{1,0:T(8,128)S(1)}, u32[]{:S(2)}, u32[]{:S(2)}) collective-permute-start(f32[256,768]{1,0:T(8,128)} %collective-permute-done.8), channel_id=1, source_target_pairs={{0,8},{8,0},{16,24},{24,16},{32,40},{40,32},{48,56},{56,48},{64,72... | collective-permute-start | bytes 2359304 | tf_op jit(solution)/shard_map/ppermute | solution.py:31
  148.8 14.9 %collective-permute-start.11 = (f32[128,768]{1,0:T(8,128)S(1)}, f32[128,768]{1,0:T(8,128)S(1)}, u32[]{:S(2)}, u32[]{:S(2)}) collective-permute-start(f32[128,768]{1,0:T(8,128)S(1)} %pad_maximum_fusion.7), channel_id=1, source_target_pairs={{0,24},{8,16},{16,8},{24,0},{32,56},{40,48},{48,40},{56,32},{64,88... | collective-permute-start | bytes 1179656 | tf_op jit(solution)/shard_map/ppermute | solution.py:31
  151.5 12.2 %collective-permute-start.7 = (f32[128,768]{1,0:T(8,128)S(1)}, f32[128,768]{1,0:T(8,128)S(1)}, u32[]{:S(2)}, u32[]{:S(2)}) collective-permute-start(f32[128,768]{1,0:T(8,128)S(1)} %pad_maximum_fusion.5), channel_id=1, source_target_pairs={{0,8},{8,0},{16,24},{24,16},{32,40},{40,32},{48,56},{56,48},{64,72... | collective-permute-start | bytes 1179656 | tf_op jit(solution)/shard_map/ppermute | solution.py:31
  (2 other events, 2.0 us)

commit v5 on v4

--- a/solution.py
+++ b/solution.py
@@ -80,7 +80,8 @@
     tg = jnp.concatenate([tok, grd], axis=0)
     tg_c = swap(after(tg, sums), CORE_SWAP)
     tg_y = swap(after(tg, tg_c), Y_SWAP)
-    part = [jnp.concatenate([act[:, k * ff : (k + 1) * ff], hg[:, k * ff : (k + 1) * ff]], axis=1) for k in range(NQ)]
+    act_, hg_ = after((act, hg), terms)
+    part = [jnp.concatenate([act_[:, k * ff : (k + 1) * ff], hg_[:, k * ff : (k + 1) * ff]], axis=1) for k in range(NQ)]
     part_y = swap(part[2], Y_SWAP)
     part_yc = swap(part[3], BOTH_SWAP)
     part_c = swap(part[1], CORE_SWAP)

time: 181 us -> 181 us (level)
  no operation moved by 1% of the time
where the time goes in v5:
time: 181 us; the launch traced here: 180 us
  blocking collectives  65 us (36%)
  starting transfers between devices  52.5 us (29%)
  waiting for transfers between devices  35.1 us (19%)
  matrix products  17.3 us (10%)
  local copies, waits for them, and re-layouts  6.17 us (3%)
  other arithmetic  3.02 us (2%)
    all_gather x1, blocking collectives, shards(): ring = lax.all_gather(both, 'dp', axis=0, axis_index_groups=Z_GROUPS)  37.9 us
    ppermute x12, starting transfers between devices, swap(): return lax.ppermute(x, 'dp', pairs)  33.7 us
    all_to_all x1, blocking collectives, sum_mp(): got = lax.all_to_all(term, 'mp', 0, 0, tiled=True)  27.1 us
    all_to_all x1, starting transfers between devices, shards(): lax.all_to_all(terms, 'dp', 0, 0, tiled=True, axis_index_groups=Z_GROUPS)  15.2 us
    ppermute x12, waiting for transfers between devices, swap(): return lax.ppermute(x, 'dp', pairs)  13.3 us
    all_to_all x1, waiting for transfers between devices, shards(): lax.all_to_all(terms, 'dp', 0, 0, tiled=True, axis_index_groups=Z_GROUPS)  11.3 us
    all_to_all x1, waiting for transfers between devices, gather_mp(): return lax.all_to_all(copies, 'mp', 0, 0, tiled=True)  10.5 us
    dot_general x5, matrix products, mm_nt(): return dot(a, b, (((1,), (1,)), ((), ())))  6.85 us
  transfers between devices with their start and end apart: 14, of which 6 were waited for; matrix products, arithmetic and copies ran while one was open for 12% of the time, Pallas kernels for 0%

profile of v5, /device:TPU:32, one launch (start us, length us, event | category | flops | bytes accessed | tf_op | source)
XLA Modules:
  0.0 180.2 jit_solution(17006470762772053559)
XLA Ops:
  0.6 5.1 %collective-permute-start.1 = (f32[768,384]{1,0:T(8,128)}, f32[768,384]{1,0:T(8,128)S(1)}, u32[]{:S(2)}, u32[]{:S(2)}) collective-permute-start(f32[768,384]{1,0:T(8,128)} %param.5), channel_id=1, source_target_pairs={{0,16},{8,24},{16,0},{24,8},{32,48},{40,56},{48,32},{56,40},{64,80... | collective-permute-start | bytes 3538952 | tf_op jit(solution)/shard_map/ppermute | solution.py:31
  5.7 1.9 %collective-permute-start = (f32[768,384]{1,0:T(8,128)}, f32[768,384]{1,0:T(8,128)S(1)}, u32[]{:S(2)}, u32[]{:S(2)}) collective-permute-start(f32[768,384]{1,0:T(8,128)} %param.5), channel_id=1, source_target_pairs={{0,8},{8,0},{16,24},{24,16},{32,40},{40,32},{48,56},{56,48},{64,72... | collective-permute-start | bytes 3538952 | tf_op jit(solution)/shard_map/ppermute | solution.py:31
  7.7 2.2 %collective-permute-start.4 = (f32[384,768]{1,0:T(8,128)}, f32[384,768]{1,0:T(8,128)S(1)}, u32[]{:S(2)}, u32[]{:S(2)}) collective-permute-start(f32[384,768]{1,0:T(8,128)} %param.6), channel_id=1, source_target_pairs={{0,16},{8,24},{16,0},{24,8},{32,48},{40,56},{48,32},{56,40},{64,80... | collective-permute-start | bytes 3538952 | tf_op jit(solution)/shard_map/ppermute | solution.py:31
  10.7 37.9 %all-gather = f32[256,768]{1,0:T(8,128)S(1)} all-gather(f32[16,768]{1,0:T(8,128)S(1)} %pad_maximum_fusion.9), channel_id=2, replica_groups={{0,32,64,96,128,160,192,224,256,288,320,352,384,416,448,480},{8,40,72,1..., dimensions={0}, use_global_device_ids=true | all-gather | bytes 835584 | tf_op jit(solution)/shard_map/all_gather | solution.py:60
  48.6 1.9 %collective-permute-start.2 = (f32[768,384]{1,0:T(8,128)S(1)}, f32[768,384]{1,0:T(8,128)S(1)}, u32[]{:S(2)}, u32[]{:S(2)}) collective-permute-start(f32[768,384]{1,0:T(8,128)S(1)} %collective-permute-done.1), channel_id=1, source_target_pairs={{0,8},{8,0},{16,24},{24,16},{32,40},{40,32},{48,56},{56,48},{64,72... | collective-permute-start | bytes 3538952 | tf_op jit(solution)/shard_map/ppermute | solution.py:31
  50.6 2.4 %collective-permute-start.3 = (f32[384,768]{1,0:T(8,128)}, f32[384,768]{1,0:T(8,128)S(1)}, u32[]{:S(2)}, u32[]{:S(2)}) collective-permute-start(f32[384,768]{1,0:T(8,128)} %param.6), channel_id=1, source_target_pairs={{0,8},{8,0},{16,24},{24,16},{32,40},{40,32},{48,56},{56,48},{64,72... | collective-permute-start | bytes 3538952 | tf_op jit(solution)/shard_map/ppermute | solution.py:31
  55.3 1.9 %collective-permute-done.4 = f32[384,768]{1,0:T(8,128)S(1)} collective-permute-done((f32[384,768]{1,0:T(8,128)}, f32[384,768]{1,0:T(8,128)S(1)}, u32[]{:S(2)}, u32[]{:S(2)}) %collective-permute-start.4) | collective-permute-done | bytes 1179680 | tf_op jit(solution)/shard_map/ppermute | solution.py:31
  57.2 1.9 %collective-permute-start.5 = (f32[384,768]{1,0:T(8,128)S(1)}, f32[384,768]{1,0:T(8,128)S(1)}, u32[]{:S(2)}, u32[]{:S(2)}) collective-permute-start(f32[384,768]{1,0:T(8,128)S(1)} %collective-permute-done.4), channel_id=1, source_target_pairs={{0,8},{8,0},{16,24},{24,16},{32,40},{40,32},{48,56},{56,48},{64,72... | collective-permute-start | bytes 3538952 | tf_op jit(solution)/shard_map/ppermute | solution.py:31
  64.5 27.1 %all_to_all.23 = f32[8,16,3072]{2,1,0:T(8,128)S(1)} all-to-all(f32[8,16,3072]{2,1,0:T(8,128)S(1)} %bitcast.43), channel_id=1, replica_groups=mesh['dp'=64,'mp'=8] {'mp'}, dimensions={0} | all-to-all | bytes 3145728 | tf_op jit(solution)/shard_map/all_to_all | solution.py:40
  93.1 3.6 %all-to-all-start.1 = ((f32[8,16,3072]{2,1,0:T(8,128)}), f32[8,16,3072]{2,1,0:T(8,128)S(1)}, u32[]{:S(2)}, u32[]{:S(2)}) async-start(f32[8,16,3072]{2,1,0:T(8,128)} %tile.2), calls=%async_computation.1 | async-start | bytes 3145728 | tf_op jit(solution)/shard_map/all_to_all | solution.py:46
  97.7 1.9 %collective-permute-start.6 = (f32[256,768]{1,0:T(8,128)}, f32[256,768]{1,0:T(8,128)S(1)}, u32[]{:S(2)}, u32[]{:S(2)}) collective-permute-start(f32[256,768]{1,0:T(8,128)} %pad_maximum_fusion), channel_id=1, source_target_pairs={{0,8},{8,0},{16,24},{24,16},{32,40},{40,32},{48,56},{56,48},{64,72... | collective-permute-start | bytes 2359304 | tf_op jit(solution)/shard_map/ppermute | solution.py:31
  99.6 2.5 %collective-permute-done.6 = f32[256,768]{1,0:T(8,128)S(1)} collective-permute-done((f32[256,768]{1,0:T(8,128)}, f32[256,768]{1,0:T(8,128)S(1)}, u32[]{:S(2)}, u32[]{:S(2)}) %collective-permute-start.6) | collective-permute-done | bytes 786464 | tf_op jit(solution)/shard_map/ppermute | solution.py:31
  102.1 4.8 %collective-permute-start.8 = (f32[256,768]{1,0:T(8,128)}, f32[256,768]{1,0:T(8,128)}, u32[]{:S(2)}, u32[]{:S(2)}) collective-permute-start(f32[256,768]{1,0:T(8,128)} %pad_maximum_fusion), channel_id=1, source_target_pairs={{0,16},{8,24},{16,0},{24,8},{32,48},{40,56},{48,32},{56,40},{64,80... | collective-permute-start | bytes 2359304 | tf_op jit(solution)/shard_map/ppermute | solution.py:31
  107.7 10.5 %all-to-all-done.1 = f32[8,16,3072]{2,1,0:T(8,128)S(1)} async-done(((f32[8,16,3072]{2,1,0:T(8,128)}), f32[8,16,3072]{2,1,0:T(8,128)S(1)}, u32[]{:S(2)}, u32[]{:S(2)}) %all-to-all-start.1) | async-done | bytes 1572896 | tf_op jit(solution)/shard_map/all_to_all | solution.py:46
  118.2 4.2 %fusion.16 = f32[16,8,768]{2,1,0:T(8,128)S(1)} fusion(f32[768,384]{1,0:T(8,128)} %copy-done.7, f32[768,384]{1,0:T(8,128)} %copy-done.3, f32[768,384]{1,0:T(8,128)} %copy-done.4, f32[768,384]{1,0:T(8,128)} %param.5, f32[128,3072]{1,0:T(8,128)S(1)} %bitcast.40), kind=kOutput, calls=%fused_computation.18 | convolution fusion | flops 909508608 | bytes 5898240 | tf_op jit(solution)/shard_map/dot_general | solution.py:23
  122.5 2.1 %fusion.19 = f32[16,8,768]{2,1,0:T(8,128)S(1)} fusion(f32[384,768]{1,0:T(8,128)S(1)} %copy-done.11, f32[384,768]{1,0:T(8,128)S(1)} %copy-done.6, f32[384,768]{1,0:T(8,128)S(1)} %copy-done.9, f32[384,768]{1,0:T(8,128)S(1)} %copy-done.2, f32[128,3072]{1,0:T(8,128)S(1)} %bitcast.41), kind=kOutput, calls=%fused_computation.19 | convolution fusion | flops 909508608 | bytes 5898240 | tf_op jit(solution)/shard_map/dot_general | solution.py:19
  125.5 15.2 %all-to-all-start.2 = ((f32[16,16,768]{2,1,0:T(8,128)}), f32[16,16,768]{2,1,0:T(8,128)S(1)}, u32[]{:S(2)}, u32[]{:S(2)}) async-start(f32[16,16,768]{2,1,0:T(8,128)} %pad_maximum_fusion.3), calls=%async_computation.2 | async-start | bytes 1572864 | tf_op jit(solution)/shard_map/all_to_all | solution.py:77
  141.0 4.8 %collective-permute-start.10 = (f32[128,768]{1,0:T(8,128)S(1)}, f32[128,768]{1,0:T(8,128)S(1)}, u32[]{:S(2)}, u32[]{:S(2)}) collective-permute-start(f32[128,768]{1,0:T(8,128)S(1)} %pad_maximum_fusion.6), channel_id=1, source_target_pairs={{0,16},{8,24},{16,0},{24,8},{32,48},{40,56},{48,32},{56,40},{64,80... | collective-permute-start | bytes 1179656 | tf_op jit(solution)/shard_map/ppermute | solution.py:31
  145.8 1.9 %collective-permute-start.9 = (f32[256,768]{1,0:T(8,128)}, f32[256,768]{1,0:T(8,128)S(1)}, u32[]{:S(2)}, u32[]{:S(2)}) collective-permute-start(f32[256,768]{1,0:T(8,128)} %collective-permute-done.8), channel_id=1, source_target_pairs={{0,8},{8,0},{16,24},{24,16},{32,40},{40,32},{48,56},{56,48},{64,72... | collective-permute-start | bytes 2359304 | tf_op jit(solution)/shard_map/ppermute | solution.py:31
  147.8 2.6 %collective-permute-start.11 = (f32[128,768]{1,0:T(8,128)S(1)}, f32[128,768]{1,0:T(8,128)S(1)}, u32[]{:S(2)}, u32[]{:S(2)}) collective-permute-start(f32[128,768]{1,0:T(8,128)S(1)} %pad_maximum_fusion.7), channel_id=1, source_target_pairs={{0,24},{8,16},{16,8},{24,0},{32,56},{40,48},{48,40},{56,32},{64,88... | collective-permute-start | bytes 1179656 | tf_op jit(solution)/shard_map/ppermute | solution.py:31
  150.5 2.1 %collective-permute-start.7 = (f32[128,768]{1,0:T(8,128)S(1)}, f32[128,768]{1,0:T(8,128)S(1)}, u32[]{:S(2)}, u32[]{:S(2)}) collective-permute-start(f32[128,768]{1,0:T(8,128)S(1)} %pad_maximum_fusion.5), channel_id=1, source_target_pairs={{0,8},{8,0},{16,24},{24,16},{32,40},{40,32},{48,56},{56,48},{64,72... | collective-permute-start | bytes 1179656 | tf_op jit(solution)/shard_map/ppermute | solution.py:31
  155.4 7.3 %collective-permute-done.11 = f32[128,768]{1,0:T(8,128)S(1)} collective-permute-done((f32[128,768]{1,0:T(8,128)S(1)}, f32[128,768]{1,0:T(8,128)S(1)}, u32[]{:S(2)}, u32[]{:S(2)}) %collective-permute-start.11) | collective-permute-done | bytes 393248 | tf_op jit(solution)/shard_map/ppermute | solution.py:31
  164.7 1.8 %convolution_add_fusion.1 = f32[768,384]{1,0:T(8,128)} fusion(f32[768,384]{1,0:T(8,128)S(1)} %fusion.23, f32[128,768]{1,0:T(8,128)S(1)} %get-tuple-element.33, f32[128,768]{1,0:T(8,128)S(1)} %copy-done, f32[256,768]{1,0:T(8,128)S(1)} %pad_maximum_fusion.4), kind=kOutput, calls=%fused_computation.17 | convolution fusion | flops 453476352 | bytes 3538944 | tf_op jit(solution)/shard_map/dot_general | solution.py:27
  168.2 11.3 %all-to-all-done.2 = f32[16,16,768]{2,1,0:T(8,128)S(1)} async-done(((f32[16,16,768]{2,1,0:T(8,128)}), f32[16,16,768]{2,1,0:T(8,128)S(1)}, u32[]{:S(2)}, u32[]{:S(2)}) %all-to-all-start.2) | async-done | bytes 786464 | tf_op jit(solution)/shard_map/all_to_all | solution.py:77
  (65 shorter events, 20.1 us)
Async XLA Ops:
  0.6 48.0 %collective-permute-start.1 = (f32[768,384]{1,0:T(8,128)}, f32[768,384]{1,0:T(8,128)S(1)}, u32[]{:S(2)}, u32[]{:S(2)}) collective-permute-start(f32[768,384]{1,0:T(8,128)} %param.5), channel_id=1, source_target_pairs={{0,16},{8,24},{16,0},{24,8},{32,48},{40,56},{48,32},{56,40},{64,80... | collective-permute-start | bytes 3538952 | tf_op jit(solution)/shard_map/ppermute | solution.py:31
  5.7 49.0 %collective-permute-start = (f32[768,384]{1,0:T(8,128)}, f32[768,384]{1,0:T(8,128)S(1)}, u32[]{:S(2)}, u32[]{:S(2)}) collective-permute-start(f32[768,384]{1,0:T(8,128)} %param.5), channel_id=1, source_target_pairs={{0,8},{8,0},{16,24},{24,16},{32,40},{40,32},{48,56},{56,48},{64,72... | collective-permute-start | bytes 3538952 | tf_op jit(solution)/shard_map/ppermute | solution.py:31
  7.7 49.6 %collective-permute-start.4 = (f32[384,768]{1,0:T(8,128)}, f32[384,768]{1,0:T(8,128)S(1)}, u32[]{:S(2)}, u32[]{:S(2)}) collective-permute-start(f32[384,768]{1,0:T(8,128)} %param.6), channel_id=1, source_target_pairs={{0,16},{8,24},{16,0},{24,8},{32,48},{40,56},{48,32},{56,40},{64,80... | collective-permute-start | bytes 3538952 | tf_op jit(solution)/shard_map/ppermute | solution.py:31
  48.6 10.5 %copy-start.3 = (f32[768,384]{1,0:T(8,128)}, f32[768,384]{1,0:T(8,128)S(1)}, u32[]{:S(2)}) copy-start(f32[768,384]{1,0:T(8,128)S(1)} %collective-permute-done.1) | copy-start | bytes 3538948
  48.6 11.1 %collective-permute-start.2 = (f32[768,384]{1,0:T(8,128)S(1)}, f32[768,384]{1,0:T(8,128)S(1)}, u32[]{:S(2)}, u32[]{:S(2)}) collective-permute-start(f32[768,384]{1,0:T(8,128)S(1)} %collective-permute-done.1), channel_id=1, source_target_pairs={{0,8},{8,0},{16,24},{24,16},{32,40},{40,32},{48,56},{56,48},{64,72... | collective-permute-start | bytes 3538952 | tf_op jit(solution)/shard_map/ppermute | solution.py:31
  50.6 11.5 %collective-permute-start.3 = (f32[384,768]{1,0:T(8,128)}, f32[384,768]{1,0:T(8,128)S(1)}, u32[]{:S(2)}, u32[]{:S(2)}) collective-permute-start(f32[384,768]{1,0:T(8,128)} %param.6), channel_id=1, source_target_pairs={{0,8},{8,0},{16,24},{24,16},{32,40},{40,32},{48,56},{56,48},{64,72... | collective-permute-start | bytes 3538952 | tf_op jit(solution)/shard_map/ppermute | solution.py:31
  54.8 4.4 %copy-start.4 = (f32[768,384]{1,0:T(8,128)}, f32[768,384]{1,0:T(8,128)S(1)}, u32[]{:S(2)}) copy-start(f32[768,384]{1,0:T(8,128)S(1)} %collective-permute-done) | copy-start | bytes 3538948
  57.2 5.5 %copy-start.5 = (f32[384,768]{1,0:T(8,128)}, f32[384,768]{1,0:T(8,128)S(1)}, u32[]{:S(2)}) copy-start(f32[384,768]{1,0:T(8,128)S(1)} %collective-permute-done.4) | copy-start | bytes 3538948
  57.2 6.2 %collective-permute-start.5 = (f32[384,768]{1,0:T(8,128)S(1)}, f32[384,768]{1,0:T(8,128)S(1)}, u32[]{:S(2)}, u32[]{:S(2)}) collective-permute-start(f32[384,768]{1,0:T(8,128)S(1)} %collective-permute-done.4), channel_id=1, source_target_pairs={{0,8},{8,0},{16,24},{24,16},{32,40},{40,32},{48,56},{56,48},{64,72... | collective-permute-start | bytes 3538952 | tf_op jit(solution)/shard_map/ppermute | solution.py:31
  59.7 1.7 copy-start.1
  59.7 2.4 %copy-start.7 = (f32[768,384]{1,0:T(8,128)}, f32[768,384]{1,0:T(8,128)S(1)}, u32[]{:S(2)}) copy-start(f32[768,384]{1,0:T(8,128)S(1)} %collective-permute-done.2) | copy-start | bytes 3538948
  62.1 1.4 copy-start.8
  93.1 25.1 %all-to-all-start.1 = ((f32[8,16,3072]{2,1,0:T(8,128)}), f32[8,16,3072]{2,1,0:T(8,128)S(1)}, u32[]{:S(2)}, u32[]{:S(2)}) async-start(f32[8,16,3072]{2,1,0:T(8,128)} %tile.2), calls=%async_computation.1 | async-start | bytes 3145728 | tf_op jit(solution)/shard_map/all_to_all | solution.py:46
  97.7 4.4 %collective-permute-start.6 = (f32[256,768]{1,0:T(8,128)}, f32[256,768]{1,0:T(8,128)S(1)}, u32[]{:S(2)}, u32[]{:S(2)}) collective-permute-start(f32[256,768]{1,0:T(8,128)} %pad_maximum_fusion), channel_id=1, source_target_pairs={{0,8},{8,0},{16,24},{24,16},{32,40},{40,32},{48,56},{56,48},{64,72... | collective-permute-start | bytes 2359304 | tf_op jit(solution)/shard_map/ppermute | solution.py:31
  102.1 43.7 %collective-permute-start.8 = (f32[256,768]{1,0:T(8,128)}, f32[256,768]{1,0:T(8,128)}, u32[]{:S(2)}, u32[]{:S(2)}) collective-permute-start(f32[256,768]{1,0:T(8,128)} %pad_maximum_fusion), channel_id=1, source_target_pairs={{0,16},{8,24},{16,0},{24,8},{32,48},{40,56},{48,32},{56,40},{64,80... | collective-permute-start | bytes 2359304 | tf_op jit(solution)/shard_map/ppermute | solution.py:31
  118.2 4.2 %copy-start.2 = (f32[384,768]{1,0:T(8,128)S(1)}, f32[384,768]{1,0:T(8,128)}, u32[]{:S(2)}) copy-start(f32[384,768]{1,0:T(8,128)} %param.6) | copy-start | bytes 3538948
  118.2 4.2 %copy-start.6 = (f32[384,768]{1,0:T(8,128)S(1)}, f32[384,768]{1,0:T(8,128)}, u32[]{:S(2)}) copy-start(f32[384,768]{1,0:T(8,128)} %copy-done.5) | copy-start | bytes 3538948
  118.2 4.2 %copy-start.9 = (f32[384,768]{1,0:T(8,128)S(1)}, f32[384,768]{1,0:T(8,128)}, u32[]{:S(2)}) copy-start(f32[384,768]{1,0:T(8,128)} %copy-done.8) | copy-start | bytes 3538948
  118.2 4.2 %copy-start.11 = (f32[384,768]{1,0:T(8,128)S(1)}, f32[384,768]{1,0:T(8,128)}, u32[]{:S(2)}) copy-start(f32[384,768]{1,0:T(8,128)} %copy-done.10) | copy-start | bytes 3538948
  125.5 54.0 %all-to-all-start.2 = ((f32[16,16,768]{2,1,0:T(8,128)}), f32[16,16,768]{2,1,0:T(8,128)S(1)}, u32[]{:S(2)}, u32[]{:S(2)}) async-start(f32[16,16,768]{2,1,0:T(8,128)} %pad_maximum_fusion.3), calls=%async_computation.2 | async-start | bytes 1572864 | tf_op jit(solution)/shard_map/all_to_all | solution.py:77
  141.0 14.4 %collective-permute-start.10 = (f32[128,768]{1,0:T(8,128)S(1)}, f32[128,768]{1,0:T(8,128)S(1)}, u32[]{:S(2)}, u32[]{:S(2)}) collective-permute-start(f32[128,768]{1,0:T(8,128)S(1)} %pad_maximum_fusion.6), channel_id=1, source_target_pairs={{0,16},{8,24},{16,0},{24,8},{32,48},{40,56},{48,32},{56,40},{64,80... | collective-permute-start | bytes 1179656 | tf_op jit(solution)/shard_map/ppermute | solution.py:31
  145.8 16.9 %collective-permute-start.9 = (f32[256,768]{1,0:T(8,128)}, f32[256,768]{1,0:T(8,128)S(1)}, u32[]{:S(2)}, u32[]{:S(2)}) collective-permute-start(f32[256,768]{1,0:T(8,128)} %collective-permute-done.8), channel_id=1, source_target_pairs={{0,8},{8,0},{16,24},{24,16},{32,40},{40,32},{48,56},{56,48},{64,72... | collective-permute-start | bytes 2359304 | tf_op jit(solution)/shard_map/ppermute | solution.py:31
  147.8 14.9 %collective-permute-start.11 = (f32[128,768]{1,0:T(8,128)S(1)}, f32[128,768]{1,0:T(8,128)S(1)}, u32[]{:S(2)}, u32[]{:S(2)}) collective-permute-start(f32[128,768]{1,0:T(8,128)S(1)} %pad_maximum_fusion.7), channel_id=1, source_target_pairs={{0,24},{8,16},{16,8},{24,0},{32,56},{40,48},{48,40},{56,32},{64,88... | collective-permute-start | bytes 1179656 | tf_op jit(solution)/shard_map/ppermute | solution.py:31
  150.5 12.2 %collective-permute-start.7 = (f32[128,768]{1,0:T(8,128)S(1)}, f32[128,768]{1,0:T(8,128)S(1)}, u32[]{:S(2)}, u32[]{:S(2)}) collective-permute-start(f32[128,768]{1,0:T(8,128)S(1)} %pad_maximum_fusion.5), channel_id=1, source_target_pairs={{0,8},{8,0},{16,24},{24,16},{32,40},{40,32},{48,56},{56,48},{64,72... | collective-permute-start | bytes 1179656 | tf_op jit(solution)/shard_map/ppermute | solution.py:31
  (2 other events, 2.0 us)
